TPU v7x, 256 devices: a whole 4x4x8 slice. The times are simulated.
256 devices in a mesh: roll: 32 (over y, x, core), mp: 8 (over z).
Axes of the slice: x: 4, y: 4, z: 8, core: 2. Of those that a mesh axis runs over, the one named last changes fastest.
Arguments:
- tokens: bfloat16 [12288, 5120], P('roll', 'mp'), may hold values from -24 to 24
- dest_shard: int32 [12288], P('roll'), may hold values from 0 to 31, as said below
- dest_offset: int32 [12288], P('roll'), may hold values from 0 to 383, as said below
- seg_lengths: int32 [32, 4], P('roll'), may hold values from 1 to 192, 384 in all within a row
- rewards: int32 [128], P('roll'), may hold values from 0 to 19
- groups: int32 [128], P('roll'), may hold values from 0 to 7, as said below
- reference_head_weight: bfloat16 [5120, 8, 640], P('roll', 'mp'), may hold values from -0.078125 to 0.078125
- policy_head_weight: bfloat16 [5120, 8, 640], P('roll', 'mp'), may hold values from -0.078125 to 0.078125
- upstream: bfloat16 [12288, 8, 384], P('roll', 'mp'), may hold values from -6 to 6
Outputs:
- grad_policy: float32 [5120, 8, 640], P('roll', 'mp')
Inputs may be any that keep to these rules, and one draw needn't show every extreme that they name: `dest_shard`: one rollout worker sends at most 24 rows to one trainer shard, and exactly 24 to some; every trainer shard receives exactly 384 rows. `dest_offset`: the rows bound for one trainer shard have distinct offsets. `groups`: every prompt has exactly 16 responses.
All inputs are finite; a program needn't handle non-finite values.
Results may differ from a plain program's by a relative error of at most 0.02.
The roundings to bfloat16 on the way count: a program that leaves them out, or rounds other values in their place, can miss the bound.
Values may be sent and summed in bfloat16 or wider, within the bound.
No kernel may reach another device: no remote copies, remote signals or barrier semaphores. Data moves between devices by JAX's collectives and lax.ppermute only.
A program may use at most 128 MiB of HBM per device.

v0:
```python
import jax
import jax.numpy as jnp
from jax import lax
from jax.experimental import pallas as pl
from jax.experimental.pallas import tpu as pltpu
from jax.sharding import Mesh
from jax.sharding import PartitionSpec as P

HEAD_WIDTH = 128
KL_WEIGHT = 1.0
MASKED_SCORE = -1e30

ROWS = 384
CHAINS = 1
CAP = 24
MODEL_BLOCK = 640
COLS = 640
CHUNK = 160
HALF = 2 * CHUNK
LANES = 384
F32 = jnp.float32
BF16 = jnp.bfloat16
I32 = jnp.int32

REWARDS, GROUPS, LENGTHS = 4, 8, 12
NOTE_HIGH, NOTE_LOW, NOTE_REWARD, NOTE_GROUP = 64, 65, 66, 70

VMEM = pl.BlockSpec(memory_space=pltpu.VMEM)
SMEM = pl.BlockSpec(memory_space=pltpu.SMEM)
HBM = pl.BlockSpec(memory_space=pltpu.HBM)
PARAMS = pltpu.CompilerParams(vmem_limit_bytes=36 * 1024 * 1024)


def iota(shape, dim):
    return lax.broadcasted_iota(I32, shape, dim)


def dot(a, b, contract=((1,), (0,))):
    return lax.dot_general(a, b, (contract, ((), ())), preferred_element_type=F32)


def fetch(pairs, semaphores):
    copies = [pltpu.make_async_copy(source, to, semaphores.at[i]) for i, (source, to) in enumerate(pairs)]
    for copy in copies:
        copy.start()
    return copies


def shift(value, axis, size, by):
    return lax.ppermute(value, axis, [(i, (i + by) % size) for i in range(size)])


def turned(value, first, by):
    pairs = []
    for y in range(4):
        for x in range(4):
            for c in range(2):
                to_y, to_x = (y, (x + by) % 4) if (c == 0) == first else ((y + by) % 4, x)
                pairs.append((8 * y + 2 * x + c, 8 * to_y + 2 * to_x + c))
    return lax.ppermute(value, ("y", "x", "c"), pairs)


def turned_place(where):
    y, x, odd = where[0], where[1], where[2]
    first = jnp.where(odd == 0, x, y)
    second = jnp.where(odd == 0, y, x)
    stride = jnp.where(odd == 0, 1, 4)
    return first, second, stride, 5 - stride


def wrapped(index, size):
    return lax.rem(index + size, size)


def route_kernel(small, keys, tokens, out, landed, semaphores):
    copy = fetch([(tokens, landed)], semaphores)[0]
    shard_row = keys[0:1, :]
    offset_row = keys[1:2, :]
    table = iota((32, ROWS), 0) == shard_row
    before = (iota((ROWS, ROWS), 0) < iota((ROWS, ROWS), 1)).astype(BF16)
    counts = dot(table.astype(BF16), before)
    rank = jnp.sum(jnp.where(table, counts, 0.0), axis=0, keepdims=True).astype(I32)
    slot = shard_row * CAP + rank
    hot = iota((32 * CAP, ROWS), 0) == slot
    lane = iota((MODEL_BLOCK, 2 * LANES), 1)
    half = (lane >= LANES).astype(I32)
    within = lane - half * LANES
    source = jnp.where(within < CHUNK, within, within + CHUNK) + CHUNK * half
    pick = (iota((MODEL_BLOCK, 2 * LANES), 0) == source) & (within < HALF)
    copy.wait()
    ordered = dot(landed[...], pick.astype(BF16)).astype(BF16)
    gathered = dot(hot.astype(BF16), ordered)
    odd = shard_row & 1
    note_lane = iota((1, 128), 1)
    common = jnp.zeros((1, 128), F32)
    for i in range(4):
        common = jnp.where(note_lane == NOTE_REWARD + i, small[REWARDS + i].astype(F32), common)
        common = jnp.where(note_lane == NOTE_GROUP + i, small[GROUPS + i].astype(F32), common)
    for core in range(2):
        place = offset_row + 1 + ROWS * (odd ^ core)
        mark = jnp.sum(jnp.where(hot, place, 0), axis=1, keepdims=True)
        high = (mark >> 4).astype(F32)
        low = (mark & 15).astype(F32)
        notes = jnp.where(note_lane == NOTE_HIGH, high, jnp.where(note_lane == NOTE_LOW, low, common))
        first = LANES * core
        plain = gathered[:, first : first + 256].astype(BF16)
        last = (gathered[:, first + 256 : first + 384] + notes).astype(BF16)
        for chip in range(16):
            rows = slice(2 * CAP * chip, 2 * CAP * (chip + 1))
            out[2 * chip + core, :, 0:256] = plain[rows]
            out[2 * chip + core, :, 256:384] = last[rows]


def route(small, keys, tokens):
    return pl.pallas_call(
        route_kernel,
        out_shape=jax.ShapeDtypeStruct((32, 2 * CAP, LANES), BF16),
        in_specs=[SMEM, VMEM, HBM],
        out_specs=VMEM,
        scratch_shapes=[pltpu.VMEM((ROWS, MODEL_BLOCK), BF16), pltpu.SemaphoreType.DMA((1,))],
        compiler_params=PARAMS,
        name="route",
    )(small, keys, tokens)


def place_kernel(arrived, *refs):
    outs, (landed, semaphores) = refs[:-2], refs[-2:]
    fetch([(arrived, landed)], semaphores)[0].wait()
    rows = landed[...].reshape(32 * 2 * CAP, LANES)
    notes = rows[:, 256:384].astype(F32)
    note_lane = iota((1, 128), 1)
    weight = jnp.where(note_lane == NOTE_HIGH, 16.0, jnp.where(note_lane == NOTE_LOW, 1.0, 0.0))
    mark = jnp.sum(notes * weight, axis=1, keepdims=True).astype(I32) - 1
    hot = (mark == iota((32 * 2 * CAP, 2 * ROWS), 1)).astype(BF16)
    block = dot(rows, hot, ((0,), (0,))).astype(BF16)
    for i, out in enumerate(outs):
        out[...] = block[i * out.shape[0] : (i + 1) * out.shape[0]]


def place(arrived):
    return pl.pallas_call(
        place_kernel,
        out_shape=(jax.ShapeDtypeStruct((HALF // CHAINS, 2 * ROWS), BF16),) * CHAINS,
        in_specs=[HBM],
        out_specs=(VMEM,) * CHAINS,
        scratch_shapes=[pltpu.VMEM((32, 2 * CAP, LANES), BF16), pltpu.SemaphoreType.DMA((1,))],
        compiler_params=PARAMS,
        name="place",
    )(arrived)


def row_advantages(reward, group, small):
    position = iota((ROWS, 128), 0)
    result = jnp.zeros((ROWS, 128), F32)
    start = 0
    for i in range(4):
        member = group == small[GROUPS + i].astype(F32)
        count = jnp.sum(jnp.where(member, 1.0, 0.0), keepdims=True)
        total = jnp.sum(jnp.where(member, reward, 0.0), keepdims=True)
        square = jnp.sum(jnp.where(member, reward * reward, 0.0), keepdims=True)
        mean = total / count
        spread = jnp.maximum(jnp.sqrt(count * square - total * total) / count, 1.0)
        advantage = (small[REWARDS + i].astype(F32) - mean) / spread
        result = jnp.where(position >= start, advantage, result)
        start = start + small[LENGTHS + i]
    return result


def gather_four(block, first):
    return [block, turned(block, first, 1), turned(block, first, -1), turned(block, first, 2)]


STEPS = (-2, -1, 0, 1, 2, 3, -3, 4)


def slot_of(chunk, z):
    at = wrapped(lax.div(chunk, 2) - z + 2, 8)
    at = jnp.where(at == 6, 7, jnp.where(at == 7, 6, at))
    return pl.multiple_of((2 * at + lax.rem(chunk, 2)) * CHUNK, 16)


def stacked(pieces, whole):
    pairs, at = [], 0
    for piece in pieces:
        pairs.append((piece, whole.at[pl.ds(at, piece.shape[0]), :]))
        at += piece.shape[0]
    return pairs


def project_kernel(where, arrived, *refs):
    tokens, pieces = refs[:-12], refs[-12:-8]
    own, other, late, advantage, whole, weights, notes, semaphores = refs[-8:]
    first, second, first_stride, second_stride = turned_place(where)
    pairs = [(arrived.at[:, 0:16, 256:384], notes), *stacked(tokens, whole)]
    steps = (0, -1, 1, 2)
    for step, piece in zip(steps, pieces):
        for k in range(4):
            chunk = wrapped(first + steps[k], 4) * first_stride + wrapped(second + step, 4) * second_stride
            slot = slot_of(chunk, where[3])
            pairs.append((piece.at[pl.ds(k * CHUNK, CHUNK), :], weights.at[pl.ds(slot, CHUNK), :]))
    copies = fetch(pairs, semaphores)
    copies[0].wait()
    note = notes[:, 0, :].astype(F32)
    advantage[...] = row_advantages(
        note[:, NOTE_REWARD : NOTE_REWARD + 4], note[:, NOTE_GROUP : NOTE_GROUP + 4], where
    )
    for copy in copies[1:]:
        copy.wait()
    late[...] = weights[5 * HALF :, :]
    result = dot(whole[...], weights[: 5 * HALF, :], ((0,), (0,)))
    own[...] = result[:ROWS]
    other[...] = result[ROWS:]


def project(where, arrived, tokens, pieces):
    shape = jax.ShapeDtypeStruct((ROWS, 2 * COLS), F32)
    late = jax.ShapeDtypeStruct((3 * HALF, 2 * COLS), BF16)
    return pl.pallas_call(
        project_kernel,
        out_shape=(shape, shape, late, jax.ShapeDtypeStruct((ROWS, 128), F32)),
        in_specs=[SMEM] + [HBM] * (5 + len(tokens)),
        out_specs=(VMEM,) * 4,
        scratch_shapes=[
            pltpu.VMEM((5 * HALF, 2 * ROWS), BF16),
            pltpu.VMEM((16 * CHUNK, 2 * COLS), BF16),
            pltpu.VMEM((32, 16, 128), BF16),
            pltpu.SemaphoreType.DMA((17 + len(tokens),)),
        ],
        compiler_params=PARAMS,
        name="project",
    )(where, arrived, *tokens, *pieces)


def add_kernel(own, other, late, *refs):
    pieces, (own_out, other_out, tokens, semaphores) = refs[:-4], refs[-4:]
    for copy in fetch(stacked(pieces, tokens), semaphores):
        copy.wait()
    result = dot(tokens[...], late[: 2 * HALF, :], ((0,), (0,)))
    own_out[...] = own[...] + result[:ROWS]
    other_out[...] = other[...] + result[ROWS:]


def add_project(own, other, late, pieces):
    shape = jax.ShapeDtypeStruct((ROWS, 2 * COLS), F32)
    return pl.pallas_call(
        add_kernel,
        out_shape=(shape, shape),
        in_specs=[VMEM] * 3 + [HBM] * len(pieces),
        out_specs=(VMEM,) * 2,
        scratch_shapes=[pltpu.VMEM((2 * HALF, 2 * ROWS), BF16), pltpu.SemaphoreType.DMA((len(pieces),))],
        compiler_params=PARAMS,
        name="add",
    )(own, other, late, *pieces)


def late_kernel(begin, other, late, first, second, out, tokens, semaphores):
    pairs = [(first, tokens.at[pl.ds(0, CHUNK), :]), (second, tokens.at[pl.ds(CHUNK, CHUNK), :])]
    for copy in fetch(pairs, semaphores):
        copy.wait()
    columns = slice(begin, begin + COLS)
    out[...] = other[:, columns] + dot(tokens[:, ROWS:], late[2 * HALF :, columns], ((0,), (0,)))


def late_project(begin, other, late, first, second):
    def kernel(*refs):
        late_kernel(begin, *refs)

    return pl.pallas_call(
        kernel,
        out_shape=jax.ShapeDtypeStruct((ROWS, COLS), F32),
        in_specs=[VMEM] * 2 + [HBM] * 2,
        out_specs=VMEM,
        scratch_shapes=[pltpu.VMEM((HALF, 2 * ROWS), BF16), pltpu.SemaphoreType.DMA((2,))],
        compiler_params=PARAMS,
        name="late",
    )(other, late, first, second)


def collect_kernel(*refs):
    tokens, (whole, semaphores) = refs[:-2], refs[-2:]
    for copy in fetch(stacked(tokens, whole), semaphores):
        copy.wait()


def collect(tokens):
    return pl.pallas_call(
        collect_kernel,
        out_shape=jax.ShapeDtypeStruct((16 * CHUNK, 2 * ROWS), BF16),
        in_specs=[HBM] * len(tokens),
        out_specs=VMEM,
        scratch_shapes=[pltpu.SemaphoreType.DMA((len(tokens),))],
        compiler_params=PARAMS,
        name="collect",
    )(*tokens)


def two_parts(value):
    high = value.astype(BF16)
    return high, (value - high.astype(F32)).astype(BF16)


def heads(value):
    return jnp.concatenate([value[:, 128 * i : 128 * (i + 1)] for i in range(3)], axis=0)


def attend(small, projection):
    key_at = iota((ROWS, ROWS), 1)
    query_at = iota((ROWS, ROWS), 0)
    begin = jnp.zeros((ROWS, 1), I32)
    row_at = iota((ROWS, 1), 0)
    start = 0
    for i in range(4):
        begin = jnp.where(row_at >= start, start, begin)
        start = start + small[LENGTHS + i]
    allowed = (key_at <= query_at) & (key_at >= begin)
    allowed = jnp.concatenate([allowed] * 3, axis=0)
    queries, keys, values = heads(projection), projection[:, 384:512], projection[:, 512:640]
    scores = dot(queries, keys, ((1,), (1,))) * HEAD_WIDTH**-0.5
    scores = jnp.where(allowed, scores, MASKED_SCORE)
    weights = jnp.exp(scores - jnp.max(scores, axis=1, keepdims=True))
    probs = weights / jnp.sum(weights, axis=1, keepdims=True)
    rounded = probs.astype(BF16)
    return queries, keys, values, probs, rounded, dot(rounded, values)


def finish(begin, own, late, first, second, received, tokens, landed, semaphores):
    pairs = [
        (first, tokens.at[pl.ds(0, CHUNK), :]),
        (second, tokens.at[pl.ds(CHUNK, CHUNK), :]),
        (received, landed),
    ]
    copies = fetch(pairs, semaphores)
    copies[0].wait()
    copies[1].wait()
    columns = slice(begin, begin + COLS)
    result = own[:, columns] + dot(tokens[:, :ROWS], late[2 * HALF :, columns], ((0,), (0,)))
    copies[2].wait()
    return (result + landed[...]).astype(BF16)


FINISH = [
    pltpu.VMEM((HALF, 2 * ROWS), BF16),
    pltpu.VMEM((ROWS, COLS), F32),
    pltpu.SemaphoreType.DMA((3,)),
]


def ref_kernel(small, own, late, first, second, received, out, *scratch):
    projection = finish(0, own, late, first, second, received, *scratch)
    out[...] = attend(small, projection)[5]


def ref_attention(small, own, late, first, second, received):
    return pl.pallas_call(
        ref_kernel,
        out_shape=jax.ShapeDtypeStruct((3 * ROWS, HEAD_WIDTH), F32),
        in_specs=[SMEM] + [VMEM] * 2 + [HBM] * 3,
        out_specs=VMEM,
        scratch_shapes=FINISH,
        compiler_params=PARAMS,
        name="ref_attention",
    )(small, own, late, first, second, received)


def two_parts(value):
    high = value.astype(BF16)
    return high, (value - high.astype(F32)).astype(BF16)


def policy_kernel(small, own, late, first, second, received, out_ref, upstream, advantage, out, *scratch):
    scale = HEAD_WIDTH**-0.5
    projection = finish(COLS, own, late, first, second, received, *scratch)
    queries, keys, values, probs, rounded, out_policy = attend(small, projection)
    weight = jnp.concatenate([advantage[...]] * 3, axis=0)
    grad_out = weight * heads(upstream[...].astype(F32)) + KL_WEIGHT * (out_policy - out_ref[...])
    high, low = two_parts(grad_out * 12288**-0.5)
    grad_values = dot(rounded, high, ((0,), (0,))) + dot(rounded, low, ((0,), (0,)))
    grad_probs = dot(high, values, ((1,), (1,))) + dot(low, values, ((1,), (1,)))
    grad_scores = probs * (grad_probs - jnp.sum(grad_probs * probs, axis=1, keepdims=True))
    high, low = two_parts(grad_scores)
    grad_query = (dot(high, keys) + dot(low, keys)) * scale
    grad_keys = (dot(high, queries, ((0,), (0,))) + dot(low, queries, ((0,), (0,)))) * scale
    for i in range(3):
        out[:, 128 * i : 128 * (i + 1)] = grad_query[ROWS * i : ROWS * (i + 1)].astype(BF16)
    out[:, 384:512] = grad_keys.astype(BF16)
    out[:, 512:640] = grad_values.astype(BF16)


def policy_attention(small, own, late, first, second, received, out_ref, upstream, advantage):
    return pl.pallas_call(
        policy_kernel,
        out_shape=jax.ShapeDtypeStruct((ROWS, COLS), BF16),
        in_specs=[SMEM] + [VMEM] * 2 + [HBM] * 3 + [VMEM] * 3,
        out_specs=VMEM,
        scratch_shapes=FINISH,
        compiler_params=PARAMS,
        name="policy_attention",
    )(small, own, late, first, second, received, out_ref, upstream, advantage)


def gradient_dot(move, where, whole, grad):
    first, _, first_stride, second_stride = turned_place(where)
    rows = []
    for k in range(4):
        chunk = wrapped(first + move, 4) * first_stride + k * second_stride
        rows.append(whole[pl.ds(slot_of(chunk, where[3]), CHUNK), :])
    return dot(jnp.concatenate(rows, axis=0), grad).astype(BF16)


PART = jax.ShapeDtypeStruct((4 * CHUNK, COLS), BF16)


def first_gradient(where, whole, own, other, move):
    def kernel(where, whole, own, other, out, grad, semaphores):
        copy = fetch([(other, grad.at[pl.ds(ROWS, ROWS), :])], semaphores)[0]
        grad[0:ROWS, :] = own[...]
        copy.wait()
        out[...] = gradient_dot(move, where, whole, grad[...])

    return pl.pallas_call(
        kernel,
        out_shape=(PART, jax.ShapeDtypeStruct((2 * ROWS, COLS), BF16)),
        in_specs=[SMEM, VMEM, VMEM, HBM],
        out_specs=(VMEM, VMEM),
        scratch_shapes=[pltpu.SemaphoreType.DMA((1,))],
        compiler_params=PARAMS,
        name="gradient",
    )(where, whole, own, other)


def next_gradient(where, whole, grad, move):
    def kernel(where, whole, grad, out):
        out[...] = gradient_dot(move, where, whole, grad[...])

    return pl.pallas_call(
        kernel,
        out_shape=PART,
        in_specs=[SMEM, VMEM, VMEM],
        out_specs=VMEM,
        compiler_params=PARAMS,
        name="gradient",
    )(where, whole, grad)


def middle_kernel(where, own, *refs):
    pieces, outs, landed, semaphores = refs[:3], refs[3:7], refs[7], refs[8]
    second = turned_place(where)[1]
    copies = fetch([(piece, landed.at[i]) for i, piece in enumerate(pieces)], semaphores)
    for copy in copies:
        copy.wait()
    for move, out in zip((0, 1, -1, 2), outs):
        at = pl.ds(pl.multiple_of(wrapped(second + move, 4) * CHUNK, 16), CHUNK)
        total = (own[at, :].astype(F32) + landed[0, at, :].astype(F32)) + (
            landed[1, at, :].astype(F32) + landed[2, at, :].astype(F32)
        )
        out[...] = total.astype(out.dtype)


def middle_sums(where, own, pieces):
    def shape(kind):
        return jax.ShapeDtypeStruct((CHUNK, COLS), kind)

    return pl.pallas_call(
        middle_kernel,
        out_shape=(shape(F32), shape(BF16), shape(BF16), shape(BF16)),
        in_specs=[SMEM, VMEM] + [HBM] * 3,
        out_specs=(VMEM,) * 4,
        scratch_shapes=[pltpu.VMEM((3, 4 * CHUNK, COLS), BF16), pltpu.SemaphoreType.DMA((3,))],
        compiler_params=PARAMS,
        name="middle",
    )(where, own, *pieces)


def final_kernel(own, *refs):
    pieces, out, landed, semaphores = refs[:3], refs[3], refs[4], refs[5]
    for copy in fetch([(piece, landed.at[i]) for i, piece in enumerate(pieces)], semaphores):
        copy.wait()
    out[:, 0, :] = (own[...] + landed[0].astype(F32)) + (landed[1].astype(F32) + landed[2].astype(F32))


def final_sums(own, pieces):
    return pl.pallas_call(
        final_kernel,
        out_shape=jax.ShapeDtypeStruct((CHUNK, 1, COLS), F32),
        in_specs=[VMEM] + [HBM] * 3,
        out_specs=VMEM,
        scratch_shapes=[pltpu.VMEM((3, CHUNK, COLS), BF16), pltpu.SemaphoreType.DMA((3,))],
        compiler_params=PARAMS,
        name="final",
    )(own, *pieces)


def body(
    tokens,
    dest_shard,
    dest_offset,
    seg_lengths,
    rewards,
    groups,
    reference_head_weight,
    policy_head_weight,
    upstream,
):
    where = jnp.stack([lax.axis_index(name).astype(I32) for name in ("y", "x", "c", "z")])
    small = jnp.concatenate([where, rewards, groups, seg_lengths[0]])
    outgoing = route(small, jnp.stack([dest_shard, dest_offset]), tokens)
    outgoing, reference_head_weight, policy_head_weight = lax.optimization_barrier(
        (outgoing, reference_head_weight, policy_head_weight)
    )
    arrived = lax.all_to_all(outgoing, ("y", "x", "c"), split_axis=0, concat_axis=0, tiled=True)

    weights = jnp.concatenate([reference_head_weight[:, 0], policy_head_weight[:, 0]], axis=1)
    near = gather_four(weights, True)
    block = place(arrived)
    block, near = lax.optimization_barrier((block, near))
    weights = gather_four(jnp.concatenate(near, axis=0), False)

    forward, backward = [block], [block]
    for _ in range(3):
        forward.append([shift(piece, "z", 8, 1) for piece in forward[-1]])
        backward.append([shift(piece, "z", 8, -1) for piece in backward[-1]])
    if CHAINS == 1:
        first = shift(forward[3][0][:CHUNK], "z", 8, 1)
        second = shift(backward[3][0][CHUNK:], "z", 8, -1)
    else:
        first = shift(forward[3][0], "z", 8, 1)
        second = shift(backward[3][1], "z", 8, -1)

    near = [*forward[2], *forward[1], *forward[0], *backward[1], *backward[2]]
    far = [*backward[3], *forward[3]]
    own, other, late, advantage = project(small, arrived, near, weights)
    own, other = add_project(own, other, late, far)
    received = []
    for begin in (0, COLS):
        part = late_project(begin, other, late, first, second)
        received.append(lax.ppermute(part, "c", [(0, 1), (1, 0)]))
    whole = collect([*near, *far, first, second])
    out_ref = ref_attention(small, own, late, first, second, received[0])
    cotangent = upstream.reshape(ROWS, 3 * HEAD_WIDTH)
    grad = policy_attention(
        small, own, late, first, second, received[1], out_ref, cotangent, advantage
    )
    grad_other = lax.ppermute(grad, "c", [(0, 1), (1, 0)])

    part, grad = first_gradient(small, whole, grad, grad_other, 2)
    parts = [turned(part, True, 2)]
    for move in (1, -1):
        parts.append(turned(next_gradient(small, whole, grad, move), True, move))
    sums = middle_sums(small, next_gradient(small, whole, grad, 0), parts)
    parts = [turned(part, False, move) for move, part in zip((1, -1, 2), sums[1:])]
    return final_sums(sums[0], parts)


def solution(mesh):
    split = Mesh(mesh.devices.reshape(4, 4, 2, 8), ("y", "x", "c", "z"))
    roll = ("y", "x", "c")
    in_specs = (
        P(roll, "z"),
        P(roll),
        P(roll),
        P(roll, None),
        P(roll),
        P(roll),
        P(roll, "z", None),
        P(roll, "z", None),
        P(roll, "z", None),
    )
    out_specs = P(roll, "z", None)
    return jax.shard_map(body, mesh=split, in_specs=in_specs, out_specs=out_specs, check_vma=False)
```

profile of v0, /device:TPU:8, one launch (start us, length us, event | category | flops | bytes accessed | tf_op | source)
XLA Modules:
  0.0 158.7 jit_solution(7631887706522273988)
XLA Ops:
  3.2 3.6 %route.1 = bf16[32,48,384]{2,1,0:T(8,128)(2,1)} custom-call(s32[16]{0:T(128)S(1)} %concatenate.9.small.where, s32[2,384]{1,0:T(2,128)S(1)} %pad_add_fusion.keys, bf16[384,640]{1,0:T(8,128)(2,1)S(1)} %copy-done), custom_call_target="tpu_custom_call" | custom-call | tf_op jit(solution)/shard_map/route/pallas_call | solution.py:115
  6.8 7.6 %all-to-all-start = ((bf16[32,48,384]{2,1,0:T(8,128)(2,1)}), bf16[32,48,384]{2,1,0:T(8,128)(2,1)S(1)}, u32[]{:S(2)}, u32[]{:S(2)}) async-start(bf16[32,48,384]{2,1,0:T(8,128)(2,1)} %route.1), calls=%async_computation | async-start | bytes 2359296 | tf_op jit(solution)/shard_map/all_to_all | solution.py:510
  15.9 1.8 %collective-permute-start.1 = (bf16[160,1280]{1,0:T(8,128)(2,1)S(1)}, bf16[160,1280]{1,0:T(8,128)(2,1)S(1)}, u32[]{:S(2)}, u32[]{:S(2)}) collective-permute-start(bf16[160,1280]{1,0:T(8,128)(2,1)S(1)} %pad_maximum_fusion), channel_id=1, source_target_pairs={{0,48},{8,200},{16,0},{24,216},{32,16},{40,232},{48,32},{56,248},{... | collective-permute-start | bytes 1228808 | tf_op jit(solution)/shard_map/ppermute | solution.py:60
  17.7 1.8 %collective-permute-start.2 = (bf16[160,1280]{1,0:T(8,128)(2,1)S(1)}, bf16[160,1280]{1,0:T(8,128)(2,1)S(1)}, u32[]{:S(2)}, u32[]{:S(2)}) collective-permute-start(bf16[160,1280]{1,0:T(8,128)(2,1)S(1)} %pad_maximum_fusion), channel_id=1, source_target_pairs={{0,32},{8,136},{16,48},{24,152},{32,0},{40,168},{48,16},{56,184},{... | collective-permute-start | bytes 1228808 | tf_op jit(solution)/shard_map/ppermute | solution.py:60
  19.5 11.2 %all-to-all-done.arrived = bf16[32,48,384]{2,1,0:T(8,128)(2,1)S(1)} async-done(((bf16[32,48,384]{2,1,0:T(8,128)(2,1)}), bf16[32,48,384]{2,1,0:T(8,128)(2,1)S(1)}, u32[]{:S(2)}, u32[]{:S(2)}) %all-to-all-start) | async-done | bytes 1179680 | tf_op jit(solution)/shard_map/all_to_all | solution.py:510
  30.7 1.8 %place.1.refs_2_ = bf16[320,768]{1,0:T(8,128)(2,1)S(1)} custom-call(bf16[32,48,384]{2,1,0:T(8,128)(2,1)S(1)} %all-to-all-done.arrived), custom_call_target="tpu_custom_call" | custom-call | tf_op jit(solution)/shard_map/place/pallas_call | solution.py:141
  32.5 2.7 %collective-permute-done = bf16[160,1280]{1,0:T(8,128)(2,1)S(1)} collective-permute-done((bf16[160,1280]{1,0:T(8,128)(2,1)S(1)}, bf16[160,1280]{1,0:T(8,128)(2,1)S(1)}, u32[]{:S(2)}, u32[]{:S(2)}) %collective-permute-start) | collective-permute-done | bytes 409632 | tf_op jit(solution)/shard_map/ppermute | solution.py:60
  35.1 5.0 %collective-permute-done.2 = bf16[160,1280]{1,0:T(8,128)(2,1)S(1)} collective-permute-done((bf16[160,1280]{1,0:T(8,128)(2,1)S(1)}, bf16[160,1280]{1,0:T(8,128)(2,1)S(1)}, u32[]{:S(2)}, u32[]{:S(2)}) %collective-permute-start.2) | collective-permute-done | bytes 409632 | tf_op jit(solution)/shard_map/ppermute | solution.py:60
  40.2 1.9 %collective-permute-start.3 = (bf16[320,768]{1,0:T(8,128)(2,1)S(1)}, bf16[320,768]{1,0:T(8,128)(2,1)S(1)}, u32[]{:S(2)}, u32[]{:S(2)}) collective-permute-start(bf16[320,768]{1,0:T(8,128)(2,1)S(1)} %place.1.refs_2_), channel_id=1, source_target_pairs={{0,1},{1,2},{2,3},{3,4},{4,5},{5,6},{6,7},{7,0},{8,9},{9,10},{10,1... | collective-permute-start | bytes 1474568 | tf_op jit(solution)/shard_map/ppermute | solution.py:50
  42.1 3.9 %collective-permute-start.5 = (bf16[320,768]{1,0:T(8,128)(2,1)S(1)}, bf16[320,768]{1,0:T(8,128)(2,1)S(1)}, u32[]{:S(2)}, u32[]{:S(2)}) collective-permute-start(bf16[320,768]{1,0:T(8,128)(2,1)S(1)} %place.1.refs_2_), channel_id=1, source_target_pairs={{0,7},{1,0},{2,1},{3,2},{4,3},{5,4},{6,5},{7,6},{8,15},{9,8},{10,9... | collective-permute-start | bytes 1474568 | tf_op jit(solution)/shard_map/ppermute | solution.py:50
  48.3 2.1 %collective-permute-start.13 = (bf16[640,1280]{1,0:T(8,128)(2,1)S(1)}, bf16[640,1280]{1,0:T(8,128)(2,1)S(1)}, u32[]{:S(2)}, u32[]{:S(2)}) collective-permute-start(bf16[640,1280]{1,0:T(8,128)(2,1)S(1)} %constant_dynamic-update-slice_fusion.refs_5_), channel_id=1, source_target_pairs={{0,128},{8,40},{16,144},{24,56},{32,160},{40,8},{48,176},{56,24},{... | collective-permute-start | bytes 4915208 | tf_op jit(solution)/shard_map/ppermute | solution.py:60
  50.4 5.2 %collective-permute-done.5.refs_3_ = bf16[320,768]{1,0:T(8,128)(2,1)S(1)} collective-permute-done((bf16[320,768]{1,0:T(8,128)(2,1)S(1)}, bf16[320,768]{1,0:T(8,128)(2,1)S(1)}, u32[]{:S(2)}, u32[]{:S(2)}) %collective-permute-start.5) | collective-permute-done | bytes 491552 | tf_op jit(solution)/shard_map/ppermute | solution.py:50
  55.6 3.7 %collective-permute-start.6 = (bf16[320,768]{1,0:T(8,128)(2,1)S(1)}, bf16[320,768]{1,0:T(8,128)(2,1)S(1)}, u32[]{:S(2)}, u32[]{:S(2)}) collective-permute-start(bf16[320,768]{1,0:T(8,128)(2,1)S(1)} %collective-permute-done.5.refs_3_), channel_id=1, source_target_pairs={{0,7},{1,0},{2,1},{3,2},{4,3},{5,4},{6,5},{7,6},{8,15},{9,8},{10,9... | collective-permute-start | bytes 1474568 | tf_op jit(solution)/shard_map/ppermute | solution.py:50
  59.3 8.6 %collective-permute-done.6.refs_4_ = bf16[320,768]{1,0:T(8,128)(2,1)S(1)} collective-permute-done((bf16[320,768]{1,0:T(8,128)(2,1)S(1)}, bf16[320,768]{1,0:T(8,128)(2,1)S(1)}, u32[]{:S(2)}, u32[]{:S(2)}) %collective-permute-start.6) | collective-permute-done | bytes 491552 | tf_op jit(solution)/shard_map/ppermute | solution.py:50
  67.9 3.7 %collective-permute-start.7 = (bf16[320,768]{1,0:T(8,128)(2,1)S(1)}, bf16[320,768]{1,0:T(8,128)(2,1)S(1)}, u32[]{:S(2)}, u32[]{:S(2)}) collective-permute-start(bf16[320,768]{1,0:T(8,128)(2,1)S(1)} %collective-permute-done.6.refs_4_), channel_id=1, source_target_pairs={{0,7},{1,0},{2,1},{3,2},{4,3},{5,4},{6,5},{7,6},{8,15},{9,8},{10,9... | collective-permute-start | bytes 1474568 | tf_op jit(solution)/shard_map/ppermute | solution.py:50
  71.6 7.7 %collective-permute-done.7.refs_5_.refs_0_ = bf16[320,768]{1,0:T(8,128)(2,1)S(1)} collective-permute-done((bf16[320,768]{1,0:T(8,128)(2,1)S(1)}, bf16[320,768]{1,0:T(8,128)(2,1)S(1)}, u32[]{:S(2)}, u32[]{:S(2)}) %collective-permute-start.7) | collective-permute-done | bytes 491552 | tf_op jit(solution)/shard_map/ppermute | solution.py:50
  79.3 3.8 %collective-permute-start.10 = (bf16[160,768]{1,0:T(8,128)(2,1)S(1)}, bf16[160,768]{1,0:T(8,128)(2,1)S(1)}, u32[]{:S(2)}, u32[]{:S(2)}) collective-permute-start(bf16[160,768]{1,0:T(8,128)(2,1)S(1)} %slice.9), channel_id=1, source_target_pairs={{0,7},{1,0},{2,1},{3,2},{4,3},{5,4},{6,5},{7,6},{8,15},{9,8},{10,9... | collective-permute-start | bytes 737288 | tf_op jit(solution)/shard_map/ppermute | solution.py:50
  83.2 3.8 %collective-permute-done.13.refs_8_ = bf16[640,1280]{1,0:T(8,128)(2,1)S(1)} collective-permute-done((bf16[640,1280]{1,0:T(8,128)(2,1)S(1)}, bf16[640,1280]{1,0:T(8,128)(2,1)S(1)}, u32[]{:S(2)}, u32[]{:S(2)}) %collective-permute-start.13) | collective-permute-done | bytes 1638432 | tf_op jit(solution)/shard_map/ppermute | solution.py:60
  87.0 11.1 %project.1 = (f32[384,1280]{1,0:T(8,128)S(1)}, f32[384,1280]{1,0:T(8,128)S(1)}, bf16[960,1280]{1,0:T(8,128)(2,1)S(1)}, f32[384,128]{1,0:T(8,128)S(1)}) custom-call(s32[16]{0:T(128)S(1)} %concatenate.9.small.where, bf16[32,48,384]{2,1,0:T(8,128)(2,1)S(1)} %all-to-all-done.arrived, bf16[320,768]{1,0:T(8,128)(2,1)S(1)} %collective-permute-done.4.refs_0_, ...), custom_call_target="tpu_custom_call" | custom-call | tf_op jit(solution)/shard_map/project/pallas_call | solution.py:218
  98.1 2.4 %add.3 = (f32[384,1280]{1,0:T(8,128)S(1)}, f32[384,1280]{1,0:T(8,128)S(1)}) custom-call(f32[384,1280]{1,0:T(8,128)S(1)} %get-tuple-element.33.own, f32[384,1280]{1,0:T(8,128)S(1)} %get-tuple-element.34.other, bf16[960,1280]{1,0:T(8,128)(2,1)S(1)} %get-tuple-element.35.late.refs_1_, bf16[320,768]{1,0:T(8,128)(2,1)S(1)} %collective-permute-done.7.refs_5_.refs_0_, ...), custom_call_target="tpu_custom_call" | custom-call | tf_op jit(solution)/shard_map/add/pallas_call | solution.py:245
  104.4 3.1 %ref_attention.1.out_ref = f32[1152,128]{1,0:T(8,128)S(1)} custom-call(s32[16]{0:T(128)S(1)} %concatenate.9.small.where, f32[384,1280]{1,0:T(8,128)S(1)} %get-tuple-element.36.own, bf16[960,1280]{1,0:T(8,128)(2,1)S(1)} %get-tuple-element.35.late.refs_1_, bf16[160,768]{1,0:T(8,128)(2,1)S(1)} %collective-permute-done.9.refs_7_.refs_2_.first, ...), custom_call_target="tpu_custom_call" | custom-call | tf_op jit(solution)/shard_map/ref_attention/pallas_call | solution.py:354
  107.5 5.2 %policy_attention.1.own = bf16[384,640]{1,0:T(8,128)(2,1)S(1)} custom-call(s32[16]{0:T(128)S(1)} %concatenate.9.small.where, f32[384,1280]{1,0:T(8,128)S(1)} %get-tuple-element.36.own, bf16[960,1280]{1,0:T(8,128)(2,1)S(1)} %get-tuple-element.35.late.refs_1_, bf16[160,768]{1,0:T(8,128)(2,1)S(1)} %collective-permute-done.9.refs_7_.refs_2_.first, ...), custom_call_target="tpu_custom_call" | custom-call | tf_op jit(solution)/shard_map/policy_attention/pallas_call | solution.py:390
  112.9 2.9 %collect.1.whole = bf16[2560,768]{1,0:T(8,128)(2,1)S(1)} custom-call(bf16[320,768]{1,0:T(8,128)(2,1)S(1)} %collective-permute-done.4.refs_0_, bf16[320,768]{1,0:T(8,128)(2,1)S(1)} %collective-permute-done.3.refs_1_, bf16[320,768]{1,0:T(8,128)(2,1)S(1)} %place.1.refs_2_, bf16[320,768]{1,0:T(8,128)(2,1)S(1)} %collective-permute-done.5.refs_3_, ...), custom_call_target="tpu_custom_call" | custom-call | tf_op jit(solution)/shard_map/collect/pallas_call | solution.py:286
  115.9 1.8 %gradient.4 = (bf16[640,640]{1,0:T(8,128)(2,1)S(1)}, bf16[768,640]{1,0:T(8,128)(2,1)S(1)}) custom-call(s32[16]{0:T(128)S(1)} %concatenate.9.small.where, bf16[2560,768]{1,0:T(8,128)(2,1)S(1)} %collect.1.whole, bf16[384,640]{1,0:T(8,128)(2,1)S(1)} %policy_attention.1.own, bf16[384,640]{1,0:T(8,128)(2,1)S(1)} %collective-permute-done.16.other), custom_call_target="tpu_custom_call" | custom-call | tf_op jit(solution)/shard_map/gradient/pallas_call | solution.py:420
  120.7 2.1 %collective-permute-start.19 = (bf16[640,640]{1,0:T(8,128)(2,1)S(1)}, bf16[640,640]{1,0:T(8,128)(2,1)S(1)}, u32[]{:S(2)}, u32[]{:S(2)}) collective-permute-start(bf16[640,640]{1,0:T(8,128)(2,1)S(1)} %gradient.7), channel_id=1, source_target_pairs={{0,48},{8,200},{16,0},{24,216},{32,16},{40,232},{48,32},{56,248},{... | collective-permute-start | bytes 2457608 | tf_op jit(solution)/shard_map/ppermute | solution.py:60
  122.8 2.6 %collective-permute-start.17 = (bf16[640,640]{1,0:T(8,128)(2,1)S(1)}, bf16[640,640]{1,0:T(8,128)(2,1)S(1)}, u32[]{:S(2)}, u32[]{:S(2)}) collective-permute-start(bf16[640,640]{1,0:T(8,128)(2,1)S(1)} %get-tuple-element.40), channel_id=1, source_target_pairs={{0,32},{8,136},{16,48},{24,152},{32,0},{40,168},{48,16},{56,184},{... | collective-permute-start | bytes 2457608 | tf_op jit(solution)/shard_map/ppermute | solution.py:60
  126.8 14.6 %collective-permute-done.19.refs_2_ = bf16[640,640]{1,0:T(8,128)(2,1)S(1)} collective-permute-done((bf16[640,640]{1,0:T(8,128)(2,1)S(1)}, bf16[640,640]{1,0:T(8,128)(2,1)S(1)}, u32[]{:S(2)}, u32[]{:S(2)}) %collective-permute-start.19) | collective-permute-done | bytes 819232 | tf_op jit(solution)/shard_map/ppermute | solution.py:60
  141.4 3.7 %collective-permute-done.18.refs_1_ = bf16[640,640]{1,0:T(8,128)(2,1)S(1)} collective-permute-done((bf16[640,640]{1,0:T(8,128)(2,1)S(1)}, bf16[640,640]{1,0:T(8,128)(2,1)S(1)}, u32[]{:S(2)}, u32[]{:S(2)}) %collective-permute-start.18) | collective-permute-done | bytes 819232 | tf_op jit(solution)/shard_map/ppermute | solution.py:60
  146.5 2.4 %collective-permute-start.21 = (bf16[160,640]{1,0:T(8,128)(2,1)S(1)}, bf16[160,640]{1,0:T(8,128)(2,1)S(1)}, u32[]{:S(2)}, u32[]{:S(2)}) collective-permute-start(bf16[160,640]{1,0:T(8,128)(2,1)S(1)} %get-tuple-element.43), channel_id=1, source_target_pairs={{0,192},{8,56},{16,208},{24,8},{32,224},{40,24},{48,240},{56,40},{... | collective-permute-start | bytes 614408 | tf_op jit(solution)/shard_map/ppermute | solution.py:60
  148.9 2.0 %collective-permute-start.22 = (bf16[160,640]{1,0:T(8,128)(2,1)S(1)}, bf16[160,640]{1,0:T(8,128)(2,1)S(1)}, u32[]{:S(2)}, u32[]{:S(2)}) collective-permute-start(bf16[160,640]{1,0:T(8,128)(2,1)S(1)} %get-tuple-element.44), channel_id=1, source_target_pairs={{0,128},{8,40},{16,144},{24,56},{32,160},{40,8},{48,176},{56,24},{... | collective-permute-start | bytes 614408 | tf_op jit(solution)/shard_map/ppermute | solution.py:60
  152.6 4.3 %collective-permute-done.22.refs_2_ = bf16[160,640]{1,0:T(8,128)(2,1)S(1)} collective-permute-done((bf16[160,640]{1,0:T(8,128)(2,1)S(1)}, bf16[160,640]{1,0:T(8,128)(2,1)S(1)}, u32[]{:S(2)}, u32[]{:S(2)}) %collective-permute-start.22) | collective-permute-done | bytes 204832 | tf_op jit(solution)/shard_map/ppermute | solution.py:60
  156.8 1.7 %final.1 = f32[160,1,640]{2,1,0:T(1,128)} custom-call(f32[160,640]{1,0:T(8,128)S(1)} %get-tuple-element.41.own, bf16[160,640]{1,0:T(8,128)(2,1)S(1)} %collective-permute-done.20.refs_0_, bf16[160,640]{1,0:T(8,128)(2,1)S(1)} %collective-permute-done.21.refs_1_, bf16[160,640]{1,0:T(8,128)(2,1)S(1)} %collective-permute-done.22.refs_2_), custom_call_target="tpu_custom_call" | custom-call | tf_op jit(solution)/shard_map/final/pallas_call | solution.py:482
  (50 shorter events, 18.6 us)
Async XLA Ops:
  2.1 1.0 copy-start
  3.2 11.2 %copy-start.2 = (bf16[160,1,640]{2,0,1:T(8,128)(2,1)S(1)}, bf16[160,1,640]{2,0,1:T(8,128)(2,1)}, u32[]{:S(2)}) copy-start(bf16[160,1,640]{2,0,1:T(8,128)(2,1)} %param.16) | copy-start | bytes 614404
  3.2 11.2 %copy-start.3 = (bf16[160,1,640]{2,0,1:T(8,128)(2,1)S(1)}, bf16[160,1,640]{2,0,1:T(8,128)(2,1)}, u32[]{:S(2)}) copy-start(bf16[160,1,640]{2,0,1:T(8,128)(2,1)} %param.15) | copy-start | bytes 614404
  6.8 23.9 %all-to-all-start = ((bf16[32,48,384]{2,1,0:T(8,128)(2,1)}), bf16[32,48,384]{2,1,0:T(8,128)(2,1)S(1)}, u32[]{:S(2)}, u32[]{:S(2)}) async-start(bf16[32,48,384]{2,1,0:T(8,128)(2,1)} %route.1), calls=%async_computation | async-start | bytes 2359296 | tf_op jit(solution)/shard_map/all_to_all | solution.py:510
  14.4 20.7 %collective-permute-start = (bf16[160,1280]{1,0:T(8,128)(2,1)S(1)}, bf16[160,1280]{1,0:T(8,128)(2,1)S(1)}, u32[]{:S(2)}, u32[]{:S(2)}) collective-permute-start(bf16[160,1280]{1,0:T(8,128)(2,1)S(1)} %pad_maximum_fusion), channel_id=1, source_target_pairs={{0,16},{8,72},{16,32},{24,88},{32,48},{40,104},{48,0},{56,120},{64... | collective-permute-start | bytes 1228808 | tf_op jit(solution)/shard_map/ppermute | solution.py:60
  15.9 19.2 %collective-permute-start.1 = (bf16[160,1280]{1,0:T(8,128)(2,1)S(1)}, bf16[160,1280]{1,0:T(8,128)(2,1)S(1)}, u32[]{:S(2)}, u32[]{:S(2)}) collective-permute-start(bf16[160,1280]{1,0:T(8,128)(2,1)S(1)} %pad_maximum_fusion), channel_id=1, source_target_pairs={{0,48},{8,200},{16,0},{24,216},{32,16},{40,232},{48,32},{56,248},{... | collective-permute-start | bytes 1228808 | tf_op jit(solution)/shard_map/ppermute | solution.py:60
  17.7 22.5 %collective-permute-start.2 = (bf16[160,1280]{1,0:T(8,128)(2,1)S(1)}, bf16[160,1280]{1,0:T(8,128)(2,1)S(1)}, u32[]{:S(2)}, u32[]{:S(2)}) collective-permute-start(bf16[160,1280]{1,0:T(8,128)(2,1)S(1)} %pad_maximum_fusion), channel_id=1, source_target_pairs={{0,32},{8,136},{16,48},{24,152},{32,0},{40,168},{48,16},{56,184},{... | collective-permute-start | bytes 1228808 | tf_op jit(solution)/shard_map/ppermute | solution.py:60
  40.2 19.1 %collective-permute-start.3 = (bf16[320,768]{1,0:T(8,128)(2,1)S(1)}, bf16[320,768]{1,0:T(8,128)(2,1)S(1)}, u32[]{:S(2)}, u32[]{:S(2)}) collective-permute-start(bf16[320,768]{1,0:T(8,128)(2,1)S(1)} %place.1.refs_2_), channel_id=1, source_target_pairs={{0,1},{1,2},{2,3},{3,4},{4,5},{5,6},{6,7},{7,0},{8,9},{9,10},{10,1... | collective-permute-start | bytes 1474568 | tf_op jit(solution)/shard_map/ppermute | solution.py:50
  42.1 13.5 %collective-permute-start.5 = (bf16[320,768]{1,0:T(8,128)(2,1)S(1)}, bf16[320,768]{1,0:T(8,128)(2,1)S(1)}, u32[]{:S(2)}, u32[]{:S(2)}) collective-permute-start(bf16[320,768]{1,0:T(8,128)(2,1)S(1)} %place.1.refs_2_), channel_id=1, source_target_pairs={{0,7},{1,0},{2,1},{3,2},{4,3},{5,4},{6,5},{7,6},{8,15},{9,8},{10,9... | collective-permute-start | bytes 1474568 | tf_op jit(solution)/shard_map/ppermute | solution.py:50
  46.2 37.0 %collective-permute-start.11 = (bf16[640,1280]{1,0:T(8,128)(2,1)S(1)}, bf16[640,1280]{1,0:T(8,128)(2,1)S(1)}, u32[]{:S(2)}, u32[]{:S(2)}) collective-permute-start(bf16[640,1280]{1,0:T(8,128)(2,1)S(1)} %constant_dynamic-update-slice_fusion.refs_5_), channel_id=1, source_target_pairs={{0,64},{8,24},{16,80},{24,40},{32,96},{40,56},{48,112},{56,8},{64,... | collective-permute-start | bytes 4915208 | tf_op jit(solution)/shard_map/ppermute | solution.py:60
  47.5 35.7 %collective-permute-start.12 = (bf16[640,1280]{1,0:T(8,128)(2,1)S(1)}, bf16[640,1280]{1,0:T(8,128)(2,1)S(1)}, u32[]{:S(2)}, u32[]{:S(2)}) collective-permute-start(bf16[640,1280]{1,0:T(8,128)(2,1)S(1)} %constant_dynamic-update-slice_fusion.refs_5_), channel_id=1, source_target_pairs={{0,192},{8,56},{16,208},{24,8},{32,224},{40,24},{48,240},{56,40},{... | collective-permute-start | bytes 4915208 | tf_op jit(solution)/shard_map/ppermute | solution.py:60
  48.3 38.7 %collective-permute-start.13 = (bf16[640,1280]{1,0:T(8,128)(2,1)S(1)}, bf16[640,1280]{1,0:T(8,128)(2,1)S(1)}, u32[]{:S(2)}, u32[]{:S(2)}) collective-permute-start(bf16[640,1280]{1,0:T(8,128)(2,1)S(1)} %constant_dynamic-update-slice_fusion.refs_5_), channel_id=1, source_target_pairs={{0,128},{8,40},{16,144},{24,56},{32,160},{40,8},{48,176},{56,24},{... | collective-permute-start | bytes 4915208 | tf_op jit(solution)/shard_map/ppermute | solution.py:60
  55.6 12.3 %collective-permute-start.6 = (bf16[320,768]{1,0:T(8,128)(2,1)S(1)}, bf16[320,768]{1,0:T(8,128)(2,1)S(1)}, u32[]{:S(2)}, u32[]{:S(2)}) collective-permute-start(bf16[320,768]{1,0:T(8,128)(2,1)S(1)} %collective-permute-done.5.refs_3_), channel_id=1, source_target_pairs={{0,7},{1,0},{2,1},{3,2},{4,3},{5,4},{6,5},{7,6},{8,15},{9,8},{10,9... | collective-permute-start | bytes 1474568 | tf_op jit(solution)/shard_map/ppermute | solution.py:50
  59.3 12.3 %collective-permute-start.4 = (bf16[320,768]{1,0:T(8,128)(2,1)S(1)}, bf16[320,768]{1,0:T(8,128)(2,1)S(1)}, u32[]{:S(2)}, u32[]{:S(2)}) collective-permute-start(bf16[320,768]{1,0:T(8,128)(2,1)S(1)} %collective-permute-done.3.refs_1_), channel_id=1, source_target_pairs={{0,1},{1,2},{2,3},{3,4},{4,5},{5,6},{6,7},{7,0},{8,9},{9,10},{10,1... | collective-permute-start | bytes 1474568 | tf_op jit(solution)/shard_map/ppermute | solution.py:50
  67.9 11.4 %collective-permute-start.7 = (bf16[320,768]{1,0:T(8,128)(2,1)S(1)}, bf16[320,768]{1,0:T(8,128)(2,1)S(1)}, u32[]{:S(2)}, u32[]{:S(2)}) collective-permute-start(bf16[320,768]{1,0:T(8,128)(2,1)S(1)} %collective-permute-done.6.refs_4_), channel_id=1, source_target_pairs={{0,7},{1,0},{2,1},{3,2},{4,3},{5,4},{6,5},{7,6},{8,15},{9,8},{10,9... | collective-permute-start | bytes 1474568 | tf_op jit(solution)/shard_map/ppermute | solution.py:50
  71.6 11.5 %collective-permute-start.8 = (bf16[320,768]{1,0:T(8,128)(2,1)S(1)}, bf16[320,768]{1,0:T(8,128)(2,1)S(1)}, u32[]{:S(2)}, u32[]{:S(2)}) collective-permute-start(bf16[320,768]{1,0:T(8,128)(2,1)S(1)} %collective-permute-done.4.refs_0_), channel_id=1, source_target_pairs={{0,1},{1,2},{2,3},{3,4},{4,5},{5,6},{6,7},{7,0},{8,9},{9,10},{10,1... | collective-permute-start | bytes 1474568 | tf_op jit(solution)/shard_map/ppermute | solution.py:50
  79.3 21.3 %collective-permute-start.10 = (bf16[160,768]{1,0:T(8,128)(2,1)S(1)}, bf16[160,768]{1,0:T(8,128)(2,1)S(1)}, u32[]{:S(2)}, u32[]{:S(2)}) collective-permute-start(bf16[160,768]{1,0:T(8,128)(2,1)S(1)} %slice.9), channel_id=1, source_target_pairs={{0,7},{1,0},{2,1},{3,2},{4,3},{5,4},{6,5},{7,6},{8,15},{9,8},{10,9... | collective-permute-start | bytes 737288 | tf_op jit(solution)/shard_map/ppermute | solution.py:50
  83.1 17.5 %collective-permute-start.9 = (bf16[160,768]{1,0:T(8,128)(2,1)S(1)}, bf16[160,768]{1,0:T(8,128)(2,1)S(1)}, u32[]{:S(2)}, u32[]{:S(2)}) collective-permute-start(bf16[160,768]{1,0:T(8,128)(2,1)S(1)} %slice.8), channel_id=1, source_target_pairs={{0,1},{1,2},{2,3},{3,4},{4,5},{5,6},{6,7},{7,0},{8,9},{9,10},{10,1... | collective-permute-start | bytes 737288 | tf_op jit(solution)/shard_map/ppermute | solution.py:50
  101.7 2.7 %collective-permute-start.15 = (f32[384,640]{1,0:T(8,128)S(1)}, f32[384,640]{1,0:T(8,128)S(1)}, u32[]{:S(2)}, u32[]{:S(2)}) collective-permute-start(f32[384,640]{1,0:T(8,128)S(1)} %late.3), channel_id=1, source_target_pairs={{0,8},{8,0},{1,9},{9,1},{2,10},{10,2},{3,11},{11,3},{4,12},{12,4},... | collective-permute-start | bytes 2949128 | tf_op jit(solution)/shard_map/ppermute | solution.py:536
  103.0 4.5 %collective-permute-start.14 = (f32[384,640]{1,0:T(8,128)S(1)}, f32[384,640]{1,0:T(8,128)S(1)}, u32[]{:S(2)}, u32[]{:S(2)}) collective-permute-start(f32[384,640]{1,0:T(8,128)S(1)} %late.2), channel_id=1, source_target_pairs={{0,8},{8,0},{1,9},{9,1},{2,10},{10,2},{3,11},{11,3},{4,12},{12,4},... | collective-permute-start | bytes 2949128 | tf_op jit(solution)/shard_map/ppermute | solution.py:536
  104.4 3.1 %copy-start.1 = (bf16[384,1,384]{2,0,1:T(8,128)(2,1)S(1)}, bf16[384,1,384]{2,0,1:T(8,128)(2,1)}, u32[]{:S(2)}) copy-start(bf16[384,1,384]{2,0,1:T(8,128)(2,1)} %param.17) | copy-start | bytes 884740
  112.7 3.1 %collective-permute-start.16 = (bf16[384,640]{1,0:T(8,128)(2,1)S(1)}, bf16[384,640]{1,0:T(8,128)(2,1)S(1)}, u32[]{:S(2)}, u32[]{:S(2)}) collective-permute-start(bf16[384,640]{1,0:T(8,128)(2,1)S(1)} %policy_attention.1.own), channel_id=1, source_target_pairs={{0,8},{8,0},{1,9},{9,1},{2,10},{10,2},{3,11},{11,3},{4,12},{12,4},... | collective-permute-start | bytes 1474568 | tf_op jit(solution)/shard_map/ppermute | solution.py:543
  120.7 20.8 %collective-permute-start.19 = (bf16[640,640]{1,0:T(8,128)(2,1)S(1)}, bf16[640,640]{1,0:T(8,128)(2,1)S(1)}, u32[]{:S(2)}, u32[]{:S(2)}) collective-permute-start(bf16[640,640]{1,0:T(8,128)(2,1)S(1)} %gradient.7), channel_id=1, source_target_pairs={{0,48},{8,200},{16,0},{24,216},{32,16},{40,232},{48,32},{56,248},{... | collective-permute-start | bytes 2457608 | tf_op jit(solution)/shard_map/ppermute | solution.py:60
  122.8 22.3 %collective-permute-start.18 = (bf16[640,640]{1,0:T(8,128)(2,1)S(1)}, bf16[640,640]{1,0:T(8,128)(2,1)S(1)}, u32[]{:S(2)}, u32[]{:S(2)}) collective-permute-start(bf16[640,640]{1,0:T(8,128)(2,1)S(1)} %gradient.6), channel_id=1, source_target_pairs={{0,16},{8,72},{16,32},{24,88},{32,48},{40,104},{48,0},{56,120},{64... | collective-permute-start | bytes 2457608 | tf_op jit(solution)/shard_map/ppermute | solution.py:60
  122.8 22.3 %collective-permute-start.17 = (bf16[640,640]{1,0:T(8,128)(2,1)S(1)}, bf16[640,640]{1,0:T(8,128)(2,1)S(1)}, u32[]{:S(2)}, u32[]{:S(2)}) collective-permute-start(bf16[640,640]{1,0:T(8,128)(2,1)S(1)} %get-tuple-element.40), channel_id=1, source_target_pairs={{0,32},{8,136},{16,48},{24,152},{32,0},{40,168},{48,16},{56,184},{... | collective-permute-start | bytes 2457608 | tf_op jit(solution)/shard_map/ppermute | solution.py:60
  146.4 6.2 %collective-permute-start.20 = (bf16[160,640]{1,0:T(8,128)(2,1)S(1)}, bf16[160,640]{1,0:T(8,128)(2,1)S(1)}, u32[]{:S(2)}, u32[]{:S(2)}) collective-permute-start(bf16[160,640]{1,0:T(8,128)(2,1)S(1)} %get-tuple-element.42), channel_id=1, source_target_pairs={{0,64},{8,24},{16,80},{24,40},{32,96},{40,56},{48,112},{56,8},{64,... | collective-permute-start | bytes 614408 | tf_op jit(solution)/shard_map/ppermute | solution.py:60
  146.5 6.1 %collective-permute-start.21 = (bf16[160,640]{1,0:T(8,128)(2,1)S(1)}, bf16[160,640]{1,0:T(8,128)(2,1)S(1)}, u32[]{:S(2)}, u32[]{:S(2)}) collective-permute-start(bf16[160,640]{1,0:T(8,128)(2,1)S(1)} %get-tuple-element.43), channel_id=1, source_target_pairs={{0,192},{8,56},{16,208},{24,8},{32,224},{40,24},{48,240},{56,40},{... | collective-permute-start | bytes 614408 | tf_op jit(solution)/shard_map/ppermute | solution.py:60
  148.9 7.9 %collective-permute-start.22 = (bf16[160,640]{1,0:T(8,128)(2,1)S(1)}, bf16[160,640]{1,0:T(8,128)(2,1)S(1)}, u32[]{:S(2)}, u32[]{:S(2)}) collective-permute-start(bf16[160,640]{1,0:T(8,128)(2,1)S(1)} %get-tuple-element.44), channel_id=1, source_target_pairs={{0,128},{8,40},{16,144},{24,56},{32,160},{40,8},{48,176},{56,24},{... | collective-permute-start | bytes 614408 | tf_op jit(solution)/shard_map/ppermute | solution.py:60
where the time goes:
time: 161 us; the launch traced here: 159 us
  waiting for transfers between devices  69 us (43%)
  starting transfers between devices  44.2 us (27%)
  Pallas kernels  41.7 us (26%)
  local copies, waits for them, and re-layouts  3.32 us (2%)
    ppermute x12, waiting for transfers between devices, turned(): return lax.ppermute(value, ('y', 'x', 'c'), pairs)  35.8 us
    ppermute x8, waiting for transfers between devices, shift(): lax.ppermute(value, axis, [(i, (i + by) % size) for i in range(size)])  21.5 us
    ppermute x12, starting transfers between devices, turned(): return lax.ppermute(value, ('y', 'x', 'c'), pairs)  18.5 us
    ppermute x8, starting transfers between devices, shift(): lax.ppermute(value, axis, [(i, (i + by) % size) for i in range(size)])  17.1 us
    all_to_all x1, waiting for transfers between devices, body(): lax.all_to_all(outgoing, ('y', 'x', 'c'), split_axis=0, concat_axis=0, ti...  11.2 us
    pallas_call x1, Pallas kernels, project(): pl.pallas_call(project_kernel, out_shape=(shape, shape, late, jax.ShapeDt...  11.1 us
    all_to_all x1, starting transfers between devices, body(): lax.all_to_all(outgoing, ('y', 'x', 'c'), split_axis=0, concat_axis=0, ti...  7.56 us
    pallas_call x1, Pallas kernels, policy_attention(): pl.pallas_call(policy_kernel, out_shape=jax.ShapeDtypeStruct((ROWS, COLS)...  5.21 us
  transfers between devices with their start and end apart: 24, of which 12 were waited for; matrix products, arithmetic and copies ran while one was open for 0% of the time, Pallas kernels for 15%

commit v1 on v0

v1 whole, which is shorter than its diff:
```python
import jax
import jax.numpy as jnp
from jax import lax
from jax.experimental import pallas as pl
from jax.experimental.pallas import tpu as pltpu
from jax.sharding import Mesh
from jax.sharding import PartitionSpec as P

HEAD_WIDTH = 128
KL_WEIGHT = 1.0
MASKED_SCORE = -1e30

ROWS = 384
CAP = 24
MODEL_BLOCK = 640
COLS = 640
CHUNK = 160
HALF = 2 * CHUNK
LANES = 384
F32 = jnp.float32
BF16 = jnp.bfloat16
I32 = jnp.int32

REWARDS, GROUPS, LENGTHS = 4, 8, 12
NOTE_HIGH, NOTE_LOW, NOTE_REWARD, NOTE_GROUP = 64, 65, 66, 70

VMEM = pl.BlockSpec(memory_space=pltpu.VMEM)
SMEM = pl.BlockSpec(memory_space=pltpu.SMEM)
HBM = pl.BlockSpec(memory_space=pltpu.HBM)
ALONE = pltpu.CompilerParams(vmem_limit_bytes=60 * 1024 * 1024)
PARAMS = pltpu.CompilerParams(vmem_limit_bytes=36 * 1024 * 1024)


def iota(shape, dim):
    return lax.broadcasted_iota(I32, shape, dim)


def dot(a, b, contract=((1,), (0,))):
    return lax.dot_general(a, b, (contract, ((), ())), preferred_element_type=F32)


def fetch(pairs, semaphores):
    copies = [pltpu.make_async_copy(source, to, semaphores.at[i]) for i, (source, to) in enumerate(pairs)]
    for copy in copies:
        copy.start()
    return copies


def shift(value, axis, size, by):
    return lax.ppermute(value, axis, [(i, (i + by) % size) for i in range(size)])


def turned(value, first, by):
    pairs = []
    for y in range(4):
        for x in range(4):
            for c in range(2):
                to_y, to_x = (y, (x + by) % 4) if (c == 0) == first else ((y + by) % 4, x)
                pairs.append((8 * y + 2 * x + c, 8 * to_y + 2 * to_x + c))
    return lax.ppermute(value, ("y", "x", "c"), pairs)


def turned_place(where):
    y, x, odd = where[0], where[1], where[2]
    first = jnp.where(odd == 0, x, y)
    second = jnp.where(odd == 0, y, x)
    stride = jnp.where(odd == 0, 1, 4)
    return first, second, stride, 5 - stride


def wrapped(index, size):
    return lax.rem(index + size, size)


def route_kernel(rewards, groups, shard, offset, tokens, out, landed, semaphores):
    copy = fetch([(tokens, landed)], semaphores)[0]
    shard_row = shard[...].reshape(1, ROWS)
    offset_row = offset[...].reshape(1, ROWS)
    table = iota((32, ROWS), 0) == shard_row
    before = (iota((ROWS, ROWS), 0) < iota((ROWS, ROWS), 1)).astype(BF16)
    counts = dot(table.astype(BF16), before)
    rank = jnp.sum(jnp.where(table, counts, 0.0), axis=0, keepdims=True).astype(I32)
    slot = shard_row * CAP + rank
    hot = iota((32 * CAP, ROWS), 0) == slot
    lane = iota((MODEL_BLOCK, 2 * LANES), 1)
    half = (lane >= LANES).astype(I32)
    within = lane - half * LANES
    source = jnp.where(within < CHUNK, within, within + CHUNK) + CHUNK * half
    pick = (iota((MODEL_BLOCK, 2 * LANES), 0) == source) & (within < HALF)
    copy.wait()
    ordered = dot(landed[...], pick.astype(BF16)).astype(BF16)
    gathered = dot(hot.astype(BF16), ordered)
    odd = shard_row & 1
    note_lane = iota((1, 128), 1)
    common = jnp.zeros((1, 128), F32)
    for i in range(4):
        common = jnp.where(note_lane == NOTE_REWARD + i, rewards[i].astype(F32), common)
        common = jnp.where(note_lane == NOTE_GROUP + i, groups[i].astype(F32), common)
    for core in range(2):
        place = offset_row + 1 + ROWS * (odd ^ core)
        mark = jnp.sum(jnp.where(hot, place, 0), axis=1, keepdims=True)
        high = (mark >> 4).astype(F32)
        low = (mark & 15).astype(F32)
        notes = jnp.where(note_lane == NOTE_HIGH, high, jnp.where(note_lane == NOTE_LOW, low, common))
        first = LANES * core
        plain = gathered[:, first : first + 256].astype(BF16)
        last = (gathered[:, first + 256 : first + 384] + notes).astype(BF16)
        for chip in range(16):
            rows = slice(2 * CAP * chip, 2 * CAP * (chip + 1))
            out[2 * chip + core, :, 0:256] = plain[rows]
            out[2 * chip + core, :, 256:384] = last[rows]


def route(rewards, groups, shard, offset, tokens):
    return pl.pallas_call(
        route_kernel,
        out_shape=jax.ShapeDtypeStruct((32, 2 * CAP, LANES), BF16),
        in_specs=[SMEM, SMEM, VMEM, VMEM, HBM],
        out_specs=VMEM,
        scratch_shapes=[pltpu.VMEM((ROWS, MODEL_BLOCK), BF16), pltpu.SemaphoreType.DMA((1,))],
        compiler_params=ALONE,
        name="route",
    )(rewards, groups, shard, offset, tokens)


def place_kernel(arrived, out, landed, semaphores):
    fetch([(arrived, landed)], semaphores)[0].wait()
    rows = landed[...].reshape(32 * 2 * CAP, LANES)
    notes = rows[:, 256:384].astype(F32)
    note_lane = iota((1, 128), 1)
    weight = jnp.where(note_lane == NOTE_HIGH, 16.0, jnp.where(note_lane == NOTE_LOW, 1.0, 0.0))
    mark = jnp.sum(notes * weight, axis=1, keepdims=True).astype(I32) - 1
    hot = (mark == iota((32 * 2 * CAP, 2 * ROWS), 1)).astype(BF16)
    out[...] = dot(rows, hot, ((0,), (0,)))[:HALF].astype(BF16)


def place(arrived):
    return pl.pallas_call(
        place_kernel,
        out_shape=jax.ShapeDtypeStruct((HALF, 2 * ROWS), BF16),
        in_specs=[HBM],
        out_specs=VMEM,
        scratch_shapes=[pltpu.VMEM((32, 2 * CAP, LANES), BF16), pltpu.SemaphoreType.DMA((1,))],
        compiler_params=PARAMS,
        name="place",
    )(arrived)


def row_advantages(reward, group, small):
    position = iota((ROWS, 128), 0)
    result = jnp.zeros((ROWS, 128), F32)
    start = 0
    for i in range(4):
        member = group == small[GROUPS + i].astype(F32)
        count = jnp.sum(jnp.where(member, 1.0, 0.0), keepdims=True)
        total = jnp.sum(jnp.where(member, reward, 0.0), keepdims=True)
        square = jnp.sum(jnp.where(member, reward * reward, 0.0), keepdims=True)
        mean = total / count
        spread = jnp.maximum(jnp.sqrt(count * square - total * total) / count, 1.0)
        advantage = (small[REWARDS + i].astype(F32) - mean) / spread
        result = jnp.where(position >= start, advantage, result)
        start = start + small[LENGTHS + i]
    return result


def join_kernel(*refs):
    pieces, (out, semaphores) = refs[:4], refs[4:]
    for copy in fetch(stacked(pieces, out), semaphores):
        copy.wait()


def join(pieces):
    return pl.pallas_call(
        join_kernel,
        out_shape=jax.ShapeDtypeStruct((4 * CHUNK, 2 * COLS), BF16),
        in_specs=[HBM] * 4,
        out_specs=VMEM,
        scratch_shapes=[pltpu.SemaphoreType.DMA((4,))],
        compiler_params=PARAMS,
        name="join",
    )(*pieces)


STEPS = (-2, -1, 0, 1, 2, 3, -3, 4)


def slot_of(chunk, z):
    at = wrapped(lax.div(chunk, 2) - z + 2, 8)
    at = jnp.where(at == 6, 7, jnp.where(at == 7, 6, at))
    return pl.multiple_of((2 * at + lax.rem(chunk, 2)) * CHUNK, 16)


def stacked(pieces, whole):
    pairs, at = [], 0
    for piece in pieces:
        pairs.append((piece, whole.at[pl.ds(at, piece.shape[0]), :]))
        at += piece.shape[0]
    return pairs


def project_kernel(where, arrived, *refs):
    tokens, pieces = refs[:7], refs[7:11]
    own, other, late, advantage, whole, weights, notes, semaphores = refs[11:]
    first, second, first_stride, second_stride = turned_place(where)
    pairs = [(arrived.at[:, 0:16, 256:384], notes)]
    steps = (0, -1, 1, 2)
    for step, piece in zip(steps, pieces):
        for k in range(4):
            near = wrapped(first + steps[k], 4)
            chunk = near * first_stride + wrapped(second + step, 4) * second_stride
            slot = slot_of(chunk, where[3])
            pairs.append((piece.at[pl.ds(k * CHUNK, CHUNK), :], weights.at[pl.ds(slot, CHUNK), :]))
    copies = fetch(pairs + stacked(tokens, whole), semaphores)
    copies[0].wait()
    note = notes[:, 0, :].astype(F32)
    advantage[...] = row_advantages(
        note[:, NOTE_REWARD : NOTE_REWARD + 4], note[:, NOTE_GROUP : NOTE_GROUP + 4], where
    )
    for copy in copies[1:]:
        copy.wait()
    late[...] = weights[7 * HALF :, :]
    own[...] = dot(whole[:, :ROWS], weights[: 7 * HALF, :], ((0,), (0,)))
    other[...] = dot(whole[:, ROWS:], weights[: 7 * HALF, :], ((0,), (0,)))


def project(where, arrived, tokens, pieces):
    shape = jax.ShapeDtypeStruct((ROWS, 2 * COLS), F32)
    late = jax.ShapeDtypeStruct((HALF, 2 * COLS), BF16)
    whole = jax.ShapeDtypeStruct((7 * HALF, 2 * ROWS), BF16)
    return pl.pallas_call(
        project_kernel,
        out_shape=(shape, shape, late, jax.ShapeDtypeStruct((ROWS, 128), F32), whole),
        in_specs=[SMEM] + [HBM] * 12,
        out_specs=(VMEM,) * 5,
        scratch_shapes=[
            pltpu.VMEM((16 * CHUNK, 2 * COLS), BF16),
            pltpu.VMEM((32, 16, 128), BF16),
            pltpu.SemaphoreType.DMA((24,)),
        ],
        compiler_params=PARAMS,
        name="project",
    )(where, arrived, *tokens, *pieces)


def first_late(other, late, first, second):
    def kernel(other, late, first, second, out, tokens, semaphores):
        for copy in fetch(stacked([first, second], tokens), semaphores):
            copy.wait()
        out[...] = other[:, :COLS] + dot(tokens[:, ROWS:], late[:, :COLS], ((0,), (0,)))

    return pl.pallas_call(
        kernel,
        out_shape=(
            jax.ShapeDtypeStruct((ROWS, COLS), F32),
            jax.ShapeDtypeStruct((HALF, 2 * ROWS), BF16),
        ),
        in_specs=[VMEM] * 2 + [HBM] * 2,
        out_specs=(VMEM,) * 2,
        scratch_shapes=[pltpu.SemaphoreType.DMA((2,))],
        compiler_params=PARAMS,
        name="late",
    )(other, late, first, second)


def second_late(other, late, tokens):
    def kernel(other, late, tokens, out):
        out[...] = other[:, COLS:] + dot(tokens[:, ROWS:], late[:, COLS:], ((0,), (0,)))

    return pl.pallas_call(
        kernel,
        out_shape=jax.ShapeDtypeStruct((ROWS, COLS), F32),
        in_specs=[VMEM] * 3,
        out_specs=VMEM,
        compiler_params=PARAMS,
        name="late",
    )(other, late, tokens)


def heads(value):
    return jnp.concatenate([value[:, 128 * i : 128 * (i + 1)] for i in range(3)], axis=0)


def attend(small, projection, block):
    first, count = 128 * block, 128 * (block + 1)
    key_at = iota((128, count), 1)
    query_at = first + iota((128, count), 0)
    row_at = first + iota((128, 1), 0)
    begin = jnp.zeros((128, 1), I32)
    start = 0
    for i in range(4):
        begin = jnp.where(row_at >= start, start, begin)
        start = start + small[LENGTHS + i]
    allowed = (key_at <= query_at) & (key_at >= begin)
    allowed = jnp.concatenate([allowed] * 3, axis=0)
    queries = heads(projection[first:count, 0:384])
    keys, values = projection[:count, 384:512], projection[:count, 512:640]
    scores = dot(queries, keys, ((1,), (1,))) * HEAD_WIDTH**-0.5
    scores = jnp.where(allowed, scores, MASKED_SCORE)
    weights = jnp.exp(scores - jnp.max(scores, axis=1, keepdims=True))
    probs = weights / jnp.sum(weights, axis=1, keepdims=True)
    rounded = probs.astype(BF16)
    return queries, keys, values, probs, rounded, dot(rounded, values)


def finish(begin, own, late, tokens, received, landed, semaphores):
    copy = fetch([(received, landed)], semaphores)[0]
    columns = slice(begin, begin + COLS)
    result = own[:, columns] + dot(tokens[:, :ROWS], late[:, columns], ((0,), (0,)))
    copy.wait()
    return (result + landed[...]).astype(BF16)


FINISH = [pltpu.VMEM((ROWS, COLS), F32), pltpu.SemaphoreType.DMA((1,))]


def ref_kernel(small, own, late, tokens, received, out, *scratch):
    projection = finish(0, own, late, tokens, received, *scratch)
    for block in range(3):
        out[ROWS * block : ROWS * (block + 1), :] = attend(small, projection, block)[5]


def ref_attention(small, own, late, tokens, received):
    return pl.pallas_call(
        ref_kernel,
        out_shape=jax.ShapeDtypeStruct((3 * ROWS, HEAD_WIDTH), F32),
        in_specs=[SMEM] + [VMEM] * 3 + [HBM],
        out_specs=VMEM,
        scratch_shapes=FINISH,
        compiler_params=PARAMS,
        name="ref_attention",
    )(small, own, late, tokens, received)


def two_parts(value):
    high = value.astype(BF16)
    return high, (value - high.astype(F32)).astype(BF16)


def policy_kernel(small, own, late, last, received, out_ref, upstream, advantage, *refs):
    out, scratch = refs[0], refs[1:]
    scale = HEAD_WIDTH**-0.5
    projection = finish(COLS, own, late, last, received, *scratch)
    grad_keys, grad_values = [0.0] * 3, [0.0] * 3
    for block in range(3):
        rows = slice(128 * block, 128 * (block + 1))
        queries, keys, values, probs, rounded, out_policy = attend(small, projection, block)
        weight = jnp.concatenate([advantage[rows, :]] * 3, axis=0)
        grad_out = weight * heads(upstream[rows, :].astype(F32))
        grad_out = grad_out + KL_WEIGHT * (out_policy - out_ref[ROWS * block : ROWS * (block + 1), :])
        high, low = two_parts(grad_out * 12288**-0.5)
        grad_probs = dot(high, values, ((1,), (1,))) + dot(low, values, ((1,), (1,)))
        grad_scores = probs * (grad_probs - jnp.sum(grad_probs * probs, axis=1, keepdims=True))
        grad_scores = (grad_scores * scale).astype(BF16)
        grad_query = dot(grad_scores, keys)
        for i in range(3):
            out[rows, 128 * i : 128 * (i + 1)] = grad_query[128 * i : 128 * (i + 1)].astype(BF16)
        for_keys = dot(grad_scores, queries, ((0,), (0,)))
        for_values = dot(rounded, high, ((0,), (0,)))
        for k in range(block + 1):
            grad_keys[k] = grad_keys[k] + for_keys[128 * k : 128 * (k + 1)]
            grad_values[k] = grad_values[k] + for_values[128 * k : 128 * (k + 1)]
    for k in range(3):
        out[128 * k : 128 * (k + 1), 384:512] = grad_keys[k].astype(BF16)
        out[128 * k : 128 * (k + 1), 512:640] = grad_values[k].astype(BF16)


def policy_attention(small, own, late, last, received, out_ref, upstream, advantage):
    return pl.pallas_call(
        policy_kernel,
        out_shape=jax.ShapeDtypeStruct((ROWS, COLS), BF16),
        in_specs=[SMEM] + [VMEM] * 3 + [HBM] + [VMEM] * 3,
        out_specs=VMEM,
        scratch_shapes=FINISH,
        compiler_params=PARAMS,
        name="policy_attention",
    )(small, own, late, last, received, out_ref, upstream, advantage)


def gradient_dot(move, where, whole, last, grad):
    first, _, first_stride, second_stride = turned_place(where)
    rows = []
    for k in range(4):
        chunk = wrapped(first + move, 4) * first_stride + k * second_stride
        slot = slot_of(chunk, where[3])
        late = slot >= 7 * HALF
        early = whole[pl.ds(pl.multiple_of(jnp.where(late, 0, slot), 16), CHUNK), :]
        later = last[pl.ds(pl.multiple_of(lax.rem(chunk, 2) * CHUNK, 16), CHUNK), :]
        rows.append(jnp.where(late, later, early))
    return dot(jnp.concatenate(rows, axis=0), grad).astype(BF16)


PART = jax.ShapeDtypeStruct((4 * CHUNK, COLS), BF16)


def first_gradient(where, whole, last, own, other, move):
    def kernel(where, whole, last, own, other, out, grad, semaphores):
        copy = fetch([(other, grad.at[pl.ds(ROWS, ROWS), :])], semaphores)[0]
        grad[0:ROWS, :] = own[...]
        copy.wait()
        out[...] = gradient_dot(move, where, whole, last, grad[...])

    return pl.pallas_call(
        kernel,
        out_shape=(PART, jax.ShapeDtypeStruct((2 * ROWS, COLS), BF16)),
        in_specs=[SMEM, VMEM, VMEM, VMEM, HBM],
        out_specs=(VMEM, VMEM),
        scratch_shapes=[pltpu.SemaphoreType.DMA((1,))],
        compiler_params=PARAMS,
        name="gradient",
    )(where, whole, last, own, other)


def next_gradient(where, whole, last, grad, move):
    def kernel(where, whole, last, grad, out):
        out[...] = gradient_dot(move, where, whole, last, grad[...])

    return pl.pallas_call(
        kernel,
        out_shape=PART,
        in_specs=[SMEM, VMEM, VMEM, VMEM],
        out_specs=VMEM,
        compiler_params=PARAMS,
        name="gradient",
    )(where, whole, last, grad)


def middle_kernel(where, own, *refs):
    pieces, outs, landed, semaphores = refs[:3], refs[3:7], refs[7], refs[8]
    second = turned_place(where)[1]
    copies = fetch([(piece, landed.at[i]) for i, piece in enumerate(pieces)], semaphores)
    for copy in copies:
        copy.wait()
    for move, out in zip((0, 1, -1, 2), outs):
        at = pl.ds(pl.multiple_of(wrapped(second + move, 4) * CHUNK, 16), CHUNK)
        total = (own[at, :].astype(F32) + landed[0, at, :].astype(F32)) + (
            landed[1, at, :].astype(F32) + landed[2, at, :].astype(F32)
        )
        out[...] = total.astype(out.dtype)


def middle_sums(where, own, pieces):
    def shape(kind):
        return jax.ShapeDtypeStruct((CHUNK, COLS), kind)

    return pl.pallas_call(
        middle_kernel,
        out_shape=(shape(F32), shape(BF16), shape(BF16), shape(BF16)),
        in_specs=[SMEM, VMEM] + [HBM] * 3,
        out_specs=(VMEM,) * 4,
        scratch_shapes=[pltpu.VMEM((3, 4 * CHUNK, COLS), BF16), pltpu.SemaphoreType.DMA((3,))],
        compiler_params=PARAMS,
        name="middle",
    )(where, own, *pieces)


def final_kernel(own, *refs):
    pieces, out, landed, semaphores = refs[:3], refs[3], refs[4], refs[5]
    for copy in fetch([(piece, landed.at[i]) for i, piece in enumerate(pieces)], semaphores):
        copy.wait()
    out[:, 0, :] = (own[...] + landed[0].astype(F32)) + (landed[1].astype(F32) + landed[2].astype(F32))


def final_sums(own, pieces):
    return pl.pallas_call(
        final_kernel,
        out_shape=jax.ShapeDtypeStruct((CHUNK, 1, COLS), F32),
        in_specs=[VMEM] + [HBM] * 3,
        out_specs=VMEM,
        scratch_shapes=[pltpu.VMEM((3, CHUNK, COLS), BF16), pltpu.SemaphoreType.DMA((3,))],
        compiler_params=PARAMS,
        name="final",
    )(own, *pieces)


def body(
    tokens,
    dest_shard,
    dest_offset,
    seg_lengths,
    rewards,
    groups,
    reference_head_weight,
    policy_head_weight,
    upstream,
):
    where = jnp.stack([lax.axis_index(name).astype(I32) for name in ("y", "x", "c", "z")])
    small = jnp.concatenate([where, rewards, groups, seg_lengths[0]])
    outgoing = route(rewards, groups, dest_shard, dest_offset, tokens)
    arrived = lax.all_to_all(outgoing, ("y", "x", "c"), split_axis=0, concat_axis=0, tiled=True)
    arrived, small = lax.optimization_barrier((arrived, small))
    _, weights, policy_weights = lax.optimization_barrier(
        (outgoing, reference_head_weight[:, 0], policy_head_weight[:, 0])
    )
    weights = jnp.concatenate([weights, policy_weights], axis=1)
    near = [weights, *(turned(weights, True, by) for by in (1, -1, 2))]
    block = place(arrived)
    _, near = lax.optimization_barrier((block, near))
    rows = join(near)
    weights = [rows, *(turned(rows, False, by) for by in (1, -1, 2))]

    forward, backward = [block], [block]
    for _ in range(3):
        forward.append(shift(forward[-1], "z", 8, 1))
        backward.append(shift(backward[-1], "z", 8, -1))

    first = shift(forward[3][:CHUNK], "z", 8, 1)
    second = shift(backward[3][CHUNK:], "z", 8, -1)
    ring = [forward[2], forward[1], block, backward[1], backward[2], backward[3], forward[3]]
    own, other, late, advantage, whole = project(small, arrived, ring, weights)
    swap = [(0, 1), (1, 0)]
    part, last = first_late(other, late, first, second)
    received_ref = lax.ppermute(part, "c", swap)
    received_policy = lax.ppermute(second_late(other, late, last), "c", swap)
    out_ref = ref_attention(small, own, late, last, received_ref)
    cotangent = upstream.reshape(ROWS, 3 * HEAD_WIDTH)
    grad = policy_attention(small, own, late, last, received_policy, out_ref, cotangent, advantage)
    grad_other = lax.ppermute(grad, "c", swap)

    part, grad = first_gradient(small, whole, last, grad, grad_other, 2)
    parts = [turned(part, True, 2)]
    for move in (1, -1):
        parts.append(turned(next_gradient(small, whole, last, grad, move), True, move))
    sums = middle_sums(small, next_gradient(small, whole, last, grad, 0), parts)
    parts = [turned(part, False, move) for move, part in zip((1, -1, 2), sums[1:])]
    return final_sums(sums[0], parts)


def solution(mesh):
    split = Mesh(mesh.devices.reshape(4, 4, 2, 8), ("y", "x", "c", "z"))
    roll = ("y", "x", "c")
    in_specs = (
        P(roll, "z"),
        P(roll),
        P(roll),
        P(roll, None),
        P(roll),
        P(roll),
        P(roll, "z", None),
        P(roll, "z", None),
        P(roll, "z", None),
    )
    out_specs = P(roll, "z", None)
    return jax.shard_map(body, mesh=split, in_specs=in_specs, out_specs=out_specs, check_vma=False)
```

time: 161 us -> 149 us (0.925)
  Pallas kernels: 41.7 us -> 37.4 us
  local copies, waits for them, and re-layouts: 3.32 us -> 0.19 us
  waiting for transfers between devices: 69 us -> 66.9 us
    ppermute x12, waiting for transfers between devices: 35.8 us -> 27.1 us  [turned(): return lax.ppermute(value, ('y', 'x', 'c'), pairs)]
    pallas_call x8 -> x7, Pallas kernels: 13.8 us -> 8.76 us  [the longest x3 4.42 us: next_gradient(): pl.pallas_call(kernel, out_shape=PART, in_specs=[SMEM, VMEM, VMEM, VMEM],...]
    ppermute x8, waiting for transfers between devices: 21.5 us -> 25.6 us  [shift(): lax.ppermute(value, axis, [(i, (i + by) % size) for i in range(size)])]
    ppermute x3, waiting for transfers between devices: 0.62 us -> 3.19 us  [the longest x1 1.73 us: body(): grad_other = lax.ppermute(grad, 'c', swap)]
  transfers between devices with their start and end apart: 24 -> 24, of which waited for: 12 -> 13; matrix products, arithmetic and copies ran while one was open for 0% -> 0% of each run, Pallas kernels for 15% -> 13%
where the time goes in v1:
time: 149 us; the launch traced here: 148 us
  waiting for transfers between devices  66.9 us (45%)
  starting transfers between devices  42.6 us (29%)
  Pallas kernels  37.4 us (25%)
    ppermute x12, waiting for transfers between devices, turned(): return lax.ppermute(value, ('y', 'x', 'c'), pairs)  27.1 us
    ppermute x8, waiting for transfers between devices, shift(): lax.ppermute(value, axis, [(i, (i + by) % size) for i in range(size)])  25.6 us
    ppermute x12, starting transfers between devices, turned(): return lax.ppermute(value, ('y', 'x', 'c'), pairs)  17.6 us
    ppermute x8, starting transfers between devices, shift(): lax.ppermute(value, axis, [(i, (i + by) % size) for i in range(size)])  16.3 us
    pallas_call x1, Pallas kernels, project(): pl.pallas_call(project_kernel, out_shape=(shape, shape, late, jax.ShapeDt...  12.7 us
    all_to_all x1, waiting for transfers between devices, body(): lax.all_to_all(outgoing, ('y', 'x', 'c'), split_axis=0, concat_axis=0, ti...  11.1 us
    all_to_all x1, starting transfers between devices, body(): lax.all_to_all(outgoing, ('y', 'x', 'c'), split_axis=0, concat_axis=0, ti...  7.68 us
    pallas_call x1, Pallas kernels, policy_attention(): pl.pallas_call(policy_kernel, out_shape=jax.ShapeDtypeStruct((ROWS, COLS)...  4.43 us
  transfers between devices with their start and end apart: 24, of which 13 were waited for; matrix products, arithmetic and copies ran while one was open for 0% of the time, Pallas kernels for 13%

profile of v1, /device:TPU:8, one launch (start us, length us, event | category | flops | bytes accessed | tf_op | source)
XLA Modules:
  0.0 147.6 jit_solution(16213075689780455237)
XLA Ops:
  0.0 4.2 %route.1 = bf16[32,48,384]{2,1,0:T(8,128)(2,1)} custom-call(s32[4]{0:T(128)} %rewards.1, s32[4]{0:T(128)} %groups.1, s32[384]{0:T(512)} %shard.1, s32[384]{0:T(512)} %offset.1, bf16[384,640]{1,0:T(8,128)(2,1)} %tokens.1), custom_call_target="tpu_custom_call" | custom-call | tf_op jit(solution)/shard_map/route/pallas_call | solution.py:115
  4.2 7.7 %all-to-all-start = ((bf16[32,48,384]{2,1,0:T(8,128)(2,1)}), bf16[32,48,384]{2,1,0:T(8,128)(2,1)S(1)}, u32[]{:S(2)}, u32[]{:S(2)}) async-start(bf16[32,48,384]{2,1,0:T(8,128)(2,1)} %route.1), calls=%async_computation | async-start | bytes 2359296 | tf_op jit(solution)/shard_map/all_to_all | solution.py:489
  12.0 1.5 %collective-permute-start.6 = (bf16[160,1280]{1,0:T(8,128)(2,1)S(1)}, bf16[160,1280]{1,0:T(8,128)(2,1)S(1)}, u32[]{:S(2)}, u32[]{:S(2)}) collective-permute-start(bf16[160,1280]{1,0:T(8,128)(2,1)S(1)} %constant_dynamic-update-slice_fusion.refs_0_), channel_id=1, source_target_pairs={{0,16},{8,72},{16,32},{24,88},{32,48},{40,104},{48,0},{56,120},{64... | collective-permute-start | bytes 1228808 | tf_op jit(solution)/shard_map/ppermute | solution.py:60
  13.6 1.8 %collective-permute-start.7 = (bf16[160,1280]{1,0:T(8,128)(2,1)S(1)}, bf16[160,1280]{1,0:T(8,128)(2,1)S(1)}, u32[]{:S(2)}, u32[]{:S(2)}) collective-permute-start(bf16[160,1280]{1,0:T(8,128)(2,1)S(1)} %constant_dynamic-update-slice_fusion.refs_0_), channel_id=1, source_target_pairs={{0,48},{8,200},{16,0},{24,216},{32,16},{40,232},{48,32},{56,248},{... | collective-permute-start | bytes 1228808 | tf_op jit(solution)/shard_map/ppermute | solution.py:60
  15.3 1.8 %collective-permute-start.8 = (bf16[160,1280]{1,0:T(8,128)(2,1)S(1)}, bf16[160,1280]{1,0:T(8,128)(2,1)S(1)}, u32[]{:S(2)}, u32[]{:S(2)}) collective-permute-start(bf16[160,1280]{1,0:T(8,128)(2,1)S(1)} %constant_dynamic-update-slice_fusion.refs_0_), channel_id=1, source_target_pairs={{0,32},{8,136},{16,48},{24,152},{32,0},{40,168},{48,16},{56,184},{... | collective-permute-start | bytes 1228808 | tf_op jit(solution)/shard_map/ppermute | solution.py:60
  17.2 11.1 %all-to-all-done.arrived = bf16[32,48,384]{2,1,0:T(8,128)(2,1)S(1)} async-done(((bf16[32,48,384]{2,1,0:T(8,128)(2,1)}), bf16[32,48,384]{2,1,0:T(8,128)(2,1)S(1)}, u32[]{:S(2)}, u32[]{:S(2)}) %all-to-all-start) | async-done | bytes 1179680 | tf_op jit(solution)/shard_map/all_to_all | solution.py:489
  28.2 1.8 %place.1.refs_2_ = bf16[320,768]{1,0:T(8,128)(2,1)S(1)} custom-call(bf16[32,48,384]{2,1,0:T(8,128)(2,1)S(1)} %all-to-all-done.arrived), custom_call_target="tpu_custom_call" | custom-call | tf_op jit(solution)/shard_map/place/pallas_call | solution.py:138
  30.1 2.0 %collective-permute-start = (bf16[320,768]{1,0:T(8,128)(2,1)S(1)}, bf16[320,768]{1,0:T(8,128)(2,1)S(1)}, u32[]{:S(2)}, u32[]{:S(2)}) collective-permute-start(bf16[320,768]{1,0:T(8,128)(2,1)S(1)} %place.1.refs_2_), channel_id=1, source_target_pairs={{0,1},{1,2},{2,3},{3,4},{4,5},{5,6},{6,7},{7,0},{8,9},{9,10},{10,1... | collective-permute-start | bytes 1474568 | tf_op jit(solution)/shard_map/ppermute | solution.py:50
  32.0 4.0 %collective-permute-start.2 = (bf16[320,768]{1,0:T(8,128)(2,1)S(1)}, bf16[320,768]{1,0:T(8,128)(2,1)S(1)}, u32[]{:S(2)}, u32[]{:S(2)}) collective-permute-start(bf16[320,768]{1,0:T(8,128)(2,1)S(1)} %place.1.refs_2_), channel_id=1, source_target_pairs={{0,7},{1,0},{2,1},{3,2},{4,3},{5,4},{6,5},{7,6},{8,15},{9,8},{10,9... | collective-permute-start | bytes 1474568 | tf_op jit(solution)/shard_map/ppermute | solution.py:50
  36.1 1.7 %collective-permute-done.8.refs_3_ = bf16[160,1280]{1,0:T(8,128)(2,1)S(1)} collective-permute-done((bf16[160,1280]{1,0:T(8,128)(2,1)S(1)}, bf16[160,1280]{1,0:T(8,128)(2,1)S(1)}, u32[]{:S(2)}, u32[]{:S(2)}) %collective-permute-start.8) | collective-permute-done | bytes 409632 | tf_op jit(solution)/shard_map/ppermute | solution.py:60
  41.4 2.0 %collective-permute-start.9 = (bf16[640,1280]{1,0:T(8,128)(2,1)S(1)}, bf16[640,1280]{1,0:T(8,128)(2,1)S(1)}, u32[]{:S(2)}, u32[]{:S(2)}) collective-permute-start(bf16[640,1280]{1,0:T(8,128)(2,1)S(1)} %join.1.refs_7_), channel_id=1, source_target_pairs={{0,64},{8,24},{16,80},{24,40},{32,96},{40,56},{48,112},{56,8},{64,... | collective-permute-start | bytes 4915208 | tf_op jit(solution)/shard_map/ppermute | solution.py:60
  43.4 4.4 %collective-permute-done.refs_1_ = bf16[320,768]{1,0:T(8,128)(2,1)S(1)} collective-permute-done((bf16[320,768]{1,0:T(8,128)(2,1)S(1)}, bf16[320,768]{1,0:T(8,128)(2,1)S(1)}, u32[]{:S(2)}, u32[]{:S(2)}) %collective-permute-start) | collective-permute-done | bytes 491552 | tf_op jit(solution)/shard_map/ppermute | solution.py:50
  47.8 3.5 %collective-permute-start.3 = (bf16[320,768]{1,0:T(8,128)(2,1)S(1)}, bf16[320,768]{1,0:T(8,128)(2,1)S(1)}, u32[]{:S(2)}, u32[]{:S(2)}) collective-permute-start(bf16[320,768]{1,0:T(8,128)(2,1)S(1)} %collective-permute-done.2.refs_3_), channel_id=1, source_target_pairs={{0,7},{1,0},{2,1},{3,2},{4,3},{5,4},{6,5},{7,6},{8,15},{9,8},{10,9... | collective-permute-start | bytes 1474568 | tf_op jit(solution)/shard_map/ppermute | solution.py:50
  51.3 11.0 %collective-permute-done.1.refs_0_ = bf16[320,768]{1,0:T(8,128)(2,1)S(1)} collective-permute-done((bf16[320,768]{1,0:T(8,128)(2,1)S(1)}, bf16[320,768]{1,0:T(8,128)(2,1)S(1)}, u32[]{:S(2)}, u32[]{:S(2)}) %collective-permute-start.1) | collective-permute-done | bytes 491552 | tf_op jit(solution)/shard_map/ppermute | solution.py:50
  62.3 3.4 %collective-permute-start.4 = (bf16[320,768]{1,0:T(8,128)(2,1)S(1)}, bf16[320,768]{1,0:T(8,128)(2,1)S(1)}, u32[]{:S(2)}, u32[]{:S(2)}) collective-permute-start(bf16[320,768]{1,0:T(8,128)(2,1)S(1)} %collective-permute-done.3.refs_4_), channel_id=1, source_target_pairs={{0,7},{1,0},{2,1},{3,2},{4,3},{5,4},{6,5},{7,6},{8,15},{9,8},{10,9... | collective-permute-start | bytes 1474568 | tf_op jit(solution)/shard_map/ppermute | solution.py:50
  65.7 10.2 %collective-permute-done.5.refs_6_ = bf16[320,768]{1,0:T(8,128)(2,1)S(1)} collective-permute-done((bf16[320,768]{1,0:T(8,128)(2,1)S(1)}, bf16[320,768]{1,0:T(8,128)(2,1)S(1)}, u32[]{:S(2)}, u32[]{:S(2)}) %collective-permute-start.5) | collective-permute-done | bytes 491552 | tf_op jit(solution)/shard_map/ppermute | solution.py:50
  76.1 3.3 %collective-permute-start.13 = (bf16[160,768]{1,0:T(8,128)(2,1)S(1)}, bf16[160,768]{1,0:T(8,128)(2,1)S(1)}, u32[]{:S(2)}, u32[]{:S(2)}) collective-permute-start(bf16[160,768]{1,0:T(8,128)(2,1)S(1)} %slice.9), channel_id=1, source_target_pairs={{0,7},{1,0},{2,1},{3,2},{4,3},{5,4},{6,5},{7,6},{8,15},{9,8},{10,9... | collective-permute-start | bytes 737288 | tf_op jit(solution)/shard_map/ppermute | solution.py:50
  79.5 12.7 %project.1 = (f32[384,1280]{1,0:T(8,128)S(1)}, f32[384,1280]{1,0:T(8,128)S(1)}, bf16[320,1280]{1,0:T(8,128)(2,1)S(1)}, f32[384,128]{1,0:T(8,128)S(1)}, bf16[2240,768]{1,0:T(8,128)(2,1)}) custom-call(s32[16]{0:T(128)S(1)} %concatenate.6.where.small, bf16[32,48,384]{2,1,0:T(8,128)(2,1)S(1)} %all-to-all-done.arrived, ...), custom_call_target="tpu_custom_call" | custom-call | tf_op jit(solution)/shard_map/project/pallas_call | solution.py:230
  96.1 2.5 %ref_attention.1.out_ref = f32[1152,128]{1,0:T(8,128)S(1)} custom-call(s32[16]{0:T(128)S(1)} %concatenate.6.where.small, f32[384,1280]{1,0:T(8,128)S(1)} %get-tuple-element.38.own, bf16[320,1280]{1,0:T(8,128)(2,1)S(1)} %get-tuple-element.36.late, bf16[320,768]{1,0:T(8,128)(2,1)S(1)} %get-tuple-element.37.tokens.last, ...), custom_call_target="tpu_custom_call" | custom-call | tf_op jit(solution)/shard_map/ref_attention/pallas_call | solution.py:323
  98.6 4.4 %policy_attention.1.own = bf16[384,640]{1,0:T(8,128)(2,1)S(1)} custom-call(s32[16]{0:T(128)S(1)} %concatenate.6.where.small, f32[384,1280]{1,0:T(8,128)S(1)} %get-tuple-element.38.own, bf16[320,1280]{1,0:T(8,128)(2,1)S(1)} %get-tuple-element.36.late, bf16[320,768]{1,0:T(8,128)(2,1)S(1)} %get-tuple-element.37.tokens.last, ...), custom_call_target="tpu_custom_call" | custom-call | tf_op jit(solution)/shard_map/policy_attention/pallas_call | solution.py:368
  103.5 1.7 %collective-permute-done.16.other = bf16[384,640]{1,0:T(8,128)(2,1)S(1)} collective-permute-done((bf16[384,640]{1,0:T(8,128)(2,1)S(1)}, bf16[384,640]{1,0:T(8,128)(2,1)S(1)}, u32[]{:S(2)}, u32[]{:S(2)}) %collective-permute-start.16) | collective-permute-done | bytes 491552 | tf_op jit(solution)/shard_map/ppermute | solution.py:517
  105.2 1.8 %gradient.4 = (bf16[640,640]{1,0:T(8,128)(2,1)S(1)}, bf16[768,640]{1,0:T(8,128)(2,1)S(1)}) custom-call(s32[16]{0:T(128)S(1)} %concatenate.6.where.small, bf16[2240,768]{1,0:T(8,128)(2,1)S(1)} %copy-done, bf16[320,768]{1,0:T(8,128)(2,1)S(1)} %get-tuple-element.37.tokens.last, bf16[384,640]{1,0:T(8,128)(2,1)S(1)} %policy_attention.1.own, ...), custom_call_target="tpu_custom_call" | custom-call | tf_op jit(solution)/shard_map/gradient/pallas_call | solution.py:402
  107.1 1.5 gradient.7
  110.0 2.1 %collective-permute-start.19 = (bf16[640,640]{1,0:T(8,128)(2,1)S(1)}, bf16[640,640]{1,0:T(8,128)(2,1)S(1)}, u32[]{:S(2)}, u32[]{:S(2)}) collective-permute-start(bf16[640,640]{1,0:T(8,128)(2,1)S(1)} %gradient.7), channel_id=1, source_target_pairs={{0,48},{8,200},{16,0},{24,216},{32,16},{40,232},{48,32},{56,248},{... | collective-permute-start | bytes 2457608 | tf_op jit(solution)/shard_map/ppermute | solution.py:60
  112.1 1.6 %collective-permute-start.17 = (bf16[640,640]{1,0:T(8,128)(2,1)S(1)}, bf16[640,640]{1,0:T(8,128)(2,1)S(1)}, u32[]{:S(2)}, u32[]{:S(2)}) collective-permute-start(bf16[640,640]{1,0:T(8,128)(2,1)S(1)} %get-tuple-element.42), channel_id=1, source_target_pairs={{0,32},{8,136},{16,48},{24,152},{32,0},{40,168},{48,16},{56,184},{... | collective-permute-start | bytes 2457608 | tf_op jit(solution)/shard_map/ppermute | solution.py:60
  115.2 15.6 %collective-permute-done.19.refs_2_ = bf16[640,640]{1,0:T(8,128)(2,1)S(1)} collective-permute-done((bf16[640,640]{1,0:T(8,128)(2,1)S(1)}, bf16[640,640]{1,0:T(8,128)(2,1)S(1)}, u32[]{:S(2)}, u32[]{:S(2)}) %collective-permute-start.19) | collective-permute-done | bytes 819232 | tf_op jit(solution)/shard_map/ppermute | solution.py:60
  130.8 3.7 %collective-permute-done.18.refs_1_ = bf16[640,640]{1,0:T(8,128)(2,1)S(1)} collective-permute-done((bf16[640,640]{1,0:T(8,128)(2,1)S(1)}, bf16[640,640]{1,0:T(8,128)(2,1)S(1)}, u32[]{:S(2)}, u32[]{:S(2)}) %collective-permute-start.18) | collective-permute-done | bytes 819232 | tf_op jit(solution)/shard_map/ppermute | solution.py:60
  136.0 1.8 %collective-permute-start.21 = (bf16[160,640]{1,0:T(8,128)(2,1)S(1)}, bf16[160,640]{1,0:T(8,128)(2,1)S(1)}, u32[]{:S(2)}, u32[]{:S(2)}) collective-permute-start(bf16[160,640]{1,0:T(8,128)(2,1)S(1)} %get-tuple-element.45), channel_id=1, source_target_pairs={{0,192},{8,56},{16,208},{24,8},{32,224},{40,24},{48,240},{56,40},{... | collective-permute-start | bytes 614408 | tf_op jit(solution)/shard_map/ppermute | solution.py:60
  137.9 1.9 %collective-permute-start.22 = (bf16[160,640]{1,0:T(8,128)(2,1)S(1)}, bf16[160,640]{1,0:T(8,128)(2,1)S(1)}, u32[]{:S(2)}, u32[]{:S(2)}) collective-permute-start(bf16[160,640]{1,0:T(8,128)(2,1)S(1)} %get-tuple-element.46), channel_id=1, source_target_pairs={{0,128},{8,40},{16,144},{24,56},{32,160},{40,8},{48,176},{56,24},{... | collective-permute-start | bytes 614408 | tf_op jit(solution)/shard_map/ppermute | solution.py:60
  139.8 1.8 %collective-permute-done.20.refs_0_ = bf16[160,640]{1,0:T(8,128)(2,1)S(1)} collective-permute-done((bf16[160,640]{1,0:T(8,128)(2,1)S(1)}, bf16[160,640]{1,0:T(8,128)(2,1)S(1)}, u32[]{:S(2)}, u32[]{:S(2)}) %collective-permute-start.20) | collective-permute-done | bytes 204832 | tf_op jit(solution)/shard_map/ppermute | solution.py:60
  141.9 3.8 %collective-permute-done.22.refs_2_ = bf16[160,640]{1,0:T(8,128)(2,1)S(1)} collective-permute-done((bf16[160,640]{1,0:T(8,128)(2,1)S(1)}, bf16[160,640]{1,0:T(8,128)(2,1)S(1)}, u32[]{:S(2)}, u32[]{:S(2)}) %collective-permute-start.22) | collective-permute-done | bytes 204832 | tf_op jit(solution)/shard_map/ppermute | solution.py:60
  145.7 1.7 %final.1 = f32[160,1,640]{2,1,0:T(1,128)} custom-call(f32[160,640]{1,0:T(8,128)S(1)} %get-tuple-element.43.own, bf16[160,640]{1,0:T(8,128)(2,1)S(1)} %collective-permute-done.20.refs_0_, bf16[160,640]{1,0:T(8,128)(2,1)S(1)} %collective-permute-done.21.refs_1_, bf16[160,640]{1,0:T(8,128)(2,1)S(1)} %collective-permute-done.22.refs_2_), custom_call_target="tpu_custom_call" | custom-call | tf_op jit(solution)/shard_map/final/pallas_call | solution.py:464
  (49 shorter events, 13.1 us)
Async XLA Ops:
  0.0 11.9 %copy-start.2 = (bf16[160,1,640]{2,0,1:T(8,128)(2,1)S(1)}, bf16[160,1,640]{2,0,1:T(8,128)(2,1)}, u32[]{:S(2)}) copy-start(bf16[160,1,640]{2,0,1:T(8,128)(2,1)} %param.15) | copy-start | bytes 614404
  4.2 7.8 %copy-start.3 = (bf16[160,1,640]{2,0,1:T(8,128)(2,1)S(1)}, bf16[160,1,640]{2,0,1:T(8,128)(2,1)}, u32[]{:S(2)}) copy-start(bf16[160,1,640]{2,0,1:T(8,128)(2,1)} %param.16) | copy-start | bytes 614404
  4.2 12.9 %copy-start.4 = (s32[4]{0:T(128)S(1)}, s32[4]{0:T(128)}, u32[]{:S(2)}) copy-start(s32[4]{0:T(128)} %rewards.1) | copy-start | bytes 52
  4.2 12.9 %copy-start.5 = (s32[4]{0:T(128)S(1)}, s32[4]{0:T(128)}, u32[]{:S(2)}) copy-start(s32[4]{0:T(128)} %groups.1) | copy-start | bytes 52
  4.2 12.9 %copy-start.6 = (s32[1,4]{1,0:T(1,128)S(1)}, s32[1,4]{1,0:T(1,128)}, u32[]{:S(2)}) copy-start(s32[1,4]{1,0:T(1,128)} %param.12) | copy-start | bytes 52
  4.2 24.0 %all-to-all-start = ((bf16[32,48,384]{2,1,0:T(8,128)(2,1)}), bf16[32,48,384]{2,1,0:T(8,128)(2,1)S(1)}, u32[]{:S(2)}, u32[]{:S(2)}) async-start(bf16[32,48,384]{2,1,0:T(8,128)(2,1)} %route.1), calls=%async_computation | async-start | bytes 2359296 | tf_op jit(solution)/shard_map/all_to_all | solution.py:489
  12.0 24.1 %collective-permute-start.6 = (bf16[160,1280]{1,0:T(8,128)(2,1)S(1)}, bf16[160,1280]{1,0:T(8,128)(2,1)S(1)}, u32[]{:S(2)}, u32[]{:S(2)}) collective-permute-start(bf16[160,1280]{1,0:T(8,128)(2,1)S(1)} %constant_dynamic-update-slice_fusion.refs_0_), channel_id=1, source_target_pairs={{0,16},{8,72},{16,32},{24,88},{32,48},{40,104},{48,0},{56,120},{64... | collective-permute-start | bytes 1228808 | tf_op jit(solution)/shard_map/ppermute | solution.py:60
  13.6 22.5 %collective-permute-start.7 = (bf16[160,1280]{1,0:T(8,128)(2,1)S(1)}, bf16[160,1280]{1,0:T(8,128)(2,1)S(1)}, u32[]{:S(2)}, u32[]{:S(2)}) collective-permute-start(bf16[160,1280]{1,0:T(8,128)(2,1)S(1)} %constant_dynamic-update-slice_fusion.refs_0_), channel_id=1, source_target_pairs={{0,48},{8,200},{16,0},{24,216},{32,16},{40,232},{48,32},{56,248},{... | collective-permute-start | bytes 1228808 | tf_op jit(solution)/shard_map/ppermute | solution.py:60
  15.3 22.5 %collective-permute-start.8 = (bf16[160,1280]{1,0:T(8,128)(2,1)S(1)}, bf16[160,1280]{1,0:T(8,128)(2,1)S(1)}, u32[]{:S(2)}, u32[]{:S(2)}) collective-permute-start(bf16[160,1280]{1,0:T(8,128)(2,1)S(1)} %constant_dynamic-update-slice_fusion.refs_0_), channel_id=1, source_target_pairs={{0,32},{8,136},{16,48},{24,152},{32,0},{40,168},{48,16},{56,184},{... | collective-permute-start | bytes 1228808 | tf_op jit(solution)/shard_map/ppermute | solution.py:60
  30.1 17.8 %collective-permute-start = (bf16[320,768]{1,0:T(8,128)(2,1)S(1)}, bf16[320,768]{1,0:T(8,128)(2,1)S(1)}, u32[]{:S(2)}, u32[]{:S(2)}) collective-permute-start(bf16[320,768]{1,0:T(8,128)(2,1)S(1)} %place.1.refs_2_), channel_id=1, source_target_pairs={{0,1},{1,2},{2,3},{3,4},{4,5},{5,6},{6,7},{7,0},{8,9},{9,10},{10,1... | collective-permute-start | bytes 1474568 | tf_op jit(solution)/shard_map/ppermute | solution.py:50
  32.0 15.8 %collective-permute-start.2 = (bf16[320,768]{1,0:T(8,128)(2,1)S(1)}, bf16[320,768]{1,0:T(8,128)(2,1)S(1)}, u32[]{:S(2)}, u32[]{:S(2)}) collective-permute-start(bf16[320,768]{1,0:T(8,128)(2,1)S(1)} %place.1.refs_2_), channel_id=1, source_target_pairs={{0,7},{1,0},{2,1},{3,2},{4,3},{5,4},{6,5},{7,6},{8,15},{9,8},{10,9... | collective-permute-start | bytes 1474568 | tf_op jit(solution)/shard_map/ppermute | solution.py:50
  38.7 40.7 %collective-permute-start.10 = (bf16[640,1280]{1,0:T(8,128)(2,1)S(1)}, bf16[640,1280]{1,0:T(8,128)(2,1)S(1)}, u32[]{:S(2)}, u32[]{:S(2)}) collective-permute-start(bf16[640,1280]{1,0:T(8,128)(2,1)S(1)} %join.1.refs_7_), channel_id=1, source_target_pairs={{0,192},{8,56},{16,208},{24,8},{32,224},{40,24},{48,240},{56,40},{... | collective-permute-start | bytes 4915208 | tf_op jit(solution)/shard_map/ppermute | solution.py:60
  40.1 39.3 %collective-permute-start.11 = (bf16[640,1280]{1,0:T(8,128)(2,1)S(1)}, bf16[640,1280]{1,0:T(8,128)(2,1)S(1)}, u32[]{:S(2)}, u32[]{:S(2)}) collective-permute-start(bf16[640,1280]{1,0:T(8,128)(2,1)S(1)} %join.1.refs_7_), channel_id=1, source_target_pairs={{0,128},{8,40},{16,144},{24,56},{32,160},{40,8},{48,176},{56,24},{... | collective-permute-start | bytes 4915208 | tf_op jit(solution)/shard_map/ppermute | solution.py:60
  41.4 38.1 %collective-permute-start.9 = (bf16[640,1280]{1,0:T(8,128)(2,1)S(1)}, bf16[640,1280]{1,0:T(8,128)(2,1)S(1)}, u32[]{:S(2)}, u32[]{:S(2)}) collective-permute-start(bf16[640,1280]{1,0:T(8,128)(2,1)S(1)} %join.1.refs_7_), channel_id=1, source_target_pairs={{0,64},{8,24},{16,80},{24,40},{32,96},{40,56},{48,112},{56,8},{64,... | collective-permute-start | bytes 4915208 | tf_op jit(solution)/shard_map/ppermute | solution.py:60
  47.8 14.5 %collective-permute-start.1 = (bf16[320,768]{1,0:T(8,128)(2,1)S(1)}, bf16[320,768]{1,0:T(8,128)(2,1)S(1)}, u32[]{:S(2)}, u32[]{:S(2)}) collective-permute-start(bf16[320,768]{1,0:T(8,128)(2,1)S(1)} %collective-permute-done.refs_1_), channel_id=1, source_target_pairs={{0,1},{1,2},{2,3},{3,4},{4,5},{5,6},{6,7},{7,0},{8,9},{9,10},{10,1... | collective-permute-start | bytes 1474568 | tf_op jit(solution)/shard_map/ppermute | solution.py:50
  47.8 14.5 %collective-permute-start.3 = (bf16[320,768]{1,0:T(8,128)(2,1)S(1)}, bf16[320,768]{1,0:T(8,128)(2,1)S(1)}, u32[]{:S(2)}, u32[]{:S(2)}) collective-permute-start(bf16[320,768]{1,0:T(8,128)(2,1)S(1)} %collective-permute-done.2.refs_3_), channel_id=1, source_target_pairs={{0,7},{1,0},{2,1},{3,2},{4,3},{5,4},{6,5},{7,6},{8,15},{9,8},{10,9... | collective-permute-start | bytes 1474568 | tf_op jit(solution)/shard_map/ppermute | solution.py:50
  62.3 13.6 %collective-permute-start.5 = (bf16[320,768]{1,0:T(8,128)(2,1)S(1)}, bf16[320,768]{1,0:T(8,128)(2,1)S(1)}, u32[]{:S(2)}, u32[]{:S(2)}) collective-permute-start(bf16[320,768]{1,0:T(8,128)(2,1)S(1)} %collective-permute-done.1.refs_0_), channel_id=1, source_target_pairs={{0,1},{1,2},{2,3},{3,4},{4,5},{5,6},{6,7},{7,0},{8,9},{9,10},{10,1... | collective-permute-start | bytes 1474568 | tf_op jit(solution)/shard_map/ppermute | solution.py:50
  62.3 13.7 %collective-permute-start.4 = (bf16[320,768]{1,0:T(8,128)(2,1)S(1)}, bf16[320,768]{1,0:T(8,128)(2,1)S(1)}, u32[]{:S(2)}, u32[]{:S(2)}) collective-permute-start(bf16[320,768]{1,0:T(8,128)(2,1)S(1)} %collective-permute-done.3.refs_4_), channel_id=1, source_target_pairs={{0,7},{1,0},{2,1},{3,2},{4,3},{5,4},{6,5},{7,6},{8,15},{9,8},{10,9... | collective-permute-start | bytes 1474568 | tf_op jit(solution)/shard_map/ppermute | solution.py:50
  75.9 16.3 %collective-permute-start.12 = (bf16[160,768]{1,0:T(8,128)(2,1)S(1)}, bf16[160,768]{1,0:T(8,128)(2,1)S(1)}, u32[]{:S(2)}, u32[]{:S(2)}) collective-permute-start(bf16[160,768]{1,0:T(8,128)(2,1)S(1)} %slice.8), channel_id=1, source_target_pairs={{0,1},{1,2},{2,3},{3,4},{4,5},{5,6},{6,7},{7,0},{8,9},{9,10},{10,1... | collective-permute-start | bytes 737288 | tf_op jit(solution)/shard_map/ppermute | solution.py:50
  76.1 16.2 %collective-permute-start.13 = (bf16[160,768]{1,0:T(8,128)(2,1)S(1)}, bf16[160,768]{1,0:T(8,128)(2,1)S(1)}, u32[]{:S(2)}, u32[]{:S(2)}) collective-permute-start(bf16[160,768]{1,0:T(8,128)(2,1)S(1)} %slice.9), channel_id=1, source_target_pairs={{0,7},{1,0},{2,1},{3,2},{4,3},{5,4},{6,5},{7,6},{8,15},{9,8},{10,9... | collective-permute-start | bytes 737288 | tf_op jit(solution)/shard_map/ppermute | solution.py:50
  93.4 2.7 %collective-permute-start.15 = (f32[384,640]{1,0:T(8,128)S(1)}, f32[384,640]{1,0:T(8,128)S(1)}, u32[]{:S(2)}, u32[]{:S(2)}) collective-permute-start(f32[384,640]{1,0:T(8,128)S(1)} %get-tuple-element.39), channel_id=1, source_target_pairs={{0,8},{8,0},{1,9},{9,1},{2,10},{10,2},{3,11},{11,3},{4,12},{12,4},... | collective-permute-start | bytes 2949128 | tf_op jit(solution)/shard_map/ppermute | solution.py:512
  94.0 4.6 %collective-permute-start.14 = (f32[384,640]{1,0:T(8,128)S(1)}, f32[384,640]{1,0:T(8,128)S(1)}, u32[]{:S(2)}, u32[]{:S(2)}) collective-permute-start(f32[384,640]{1,0:T(8,128)S(1)} %late.3), channel_id=1, source_target_pairs={{0,8},{8,0},{1,9},{9,1},{2,10},{10,2},{3,11},{11,3},{4,12},{12,4},... | collective-permute-start | bytes 2949128 | tf_op jit(solution)/shard_map/ppermute | solution.py:513
  96.1 2.5 %copy-start.1 = (bf16[384,1,384]{2,0,1:T(8,128)(2,1)S(1)}, bf16[384,1,384]{2,0,1:T(8,128)(2,1)}, u32[]{:S(2)}) copy-start(bf16[384,1,384]{2,0,1:T(8,128)(2,1)} %param.17) | copy-start | bytes 884740
  98.6 6.6 %copy-start = (bf16[2240,768]{1,0:T(8,128)(2,1)S(1)}, bf16[2240,768]{1,0:T(8,128)(2,1)}, u32[]{:S(2)}) copy-start(bf16[2240,768]{1,0:T(8,128)(2,1)} %get-tuple-element.34.whole) | copy-start | bytes 10321924
  103.0 2.2 %collective-permute-start.16 = (bf16[384,640]{1,0:T(8,128)(2,1)S(1)}, bf16[384,640]{1,0:T(8,128)(2,1)S(1)}, u32[]{:S(2)}, u32[]{:S(2)}) collective-permute-start(bf16[384,640]{1,0:T(8,128)(2,1)S(1)} %policy_attention.1.own), channel_id=1, source_target_pairs={{0,8},{8,0},{1,9},{9,1},{2,10},{10,2},{3,11},{11,3},{4,12},{12,4},... | collective-permute-start | bytes 1474568 | tf_op jit(solution)/shard_map/ppermute | solution.py:517
  110.0 20.8 %collective-permute-start.19 = (bf16[640,640]{1,0:T(8,128)(2,1)S(1)}, bf16[640,640]{1,0:T(8,128)(2,1)S(1)}, u32[]{:S(2)}, u32[]{:S(2)}) collective-permute-start(bf16[640,640]{1,0:T(8,128)(2,1)S(1)} %gradient.7), channel_id=1, source_target_pairs={{0,48},{8,200},{16,0},{24,216},{32,16},{40,232},{48,32},{56,248},{... | collective-permute-start | bytes 2457608 | tf_op jit(solution)/shard_map/ppermute | solution.py:60
  112.1 22.3 %collective-permute-start.18 = (bf16[640,640]{1,0:T(8,128)(2,1)S(1)}, bf16[640,640]{1,0:T(8,128)(2,1)S(1)}, u32[]{:S(2)}, u32[]{:S(2)}) collective-permute-start(bf16[640,640]{1,0:T(8,128)(2,1)S(1)} %gradient.6), channel_id=1, source_target_pairs={{0,16},{8,72},{16,32},{24,88},{32,48},{40,104},{48,0},{56,120},{64... | collective-permute-start | bytes 2457608 | tf_op jit(solution)/shard_map/ppermute | solution.py:60
  112.1 22.3 %collective-permute-start.17 = (bf16[640,640]{1,0:T(8,128)(2,1)S(1)}, bf16[640,640]{1,0:T(8,128)(2,1)S(1)}, u32[]{:S(2)}, u32[]{:S(2)}) collective-permute-start(bf16[640,640]{1,0:T(8,128)(2,1)S(1)} %get-tuple-element.42), channel_id=1, source_target_pairs={{0,32},{8,136},{16,48},{24,152},{32,0},{40,168},{48,16},{56,184},{... | collective-permute-start | bytes 2457608 | tf_op jit(solution)/shard_map/ppermute | solution.py:60
  135.7 5.8 %collective-permute-start.20 = (bf16[160,640]{1,0:T(8,128)(2,1)S(1)}, bf16[160,640]{1,0:T(8,128)(2,1)S(1)}, u32[]{:S(2)}, u32[]{:S(2)}) collective-permute-start(bf16[160,640]{1,0:T(8,128)(2,1)S(1)} %get-tuple-element.44), channel_id=1, source_target_pairs={{0,64},{8,24},{16,80},{24,40},{32,96},{40,56},{48,112},{56,8},{64,... | collective-permute-start | bytes 614408 | tf_op jit(solution)/shard_map/ppermute | solution.py:60
  136.0 5.9 %collective-permute-start.21 = (bf16[160,640]{1,0:T(8,128)(2,1)S(1)}, bf16[160,640]{1,0:T(8,128)(2,1)S(1)}, u32[]{:S(2)}, u32[]{:S(2)}) collective-permute-start(bf16[160,640]{1,0:T(8,128)(2,1)S(1)} %get-tuple-element.45), channel_id=1, source_target_pairs={{0,192},{8,56},{16,208},{24,8},{32,224},{40,24},{48,240},{56,40},{... | collective-permute-start | bytes 614408 | tf_op jit(solution)/shard_map/ppermute | solution.py:60
  137.9 7.9 %collective-permute-start.22 = (bf16[160,640]{1,0:T(8,128)(2,1)S(1)}, bf16[160,640]{1,0:T(8,128)(2,1)S(1)}, u32[]{:S(2)}, u32[]{:S(2)}) collective-permute-start(bf16[160,640]{1,0:T(8,128)(2,1)S(1)} %get-tuple-element.46), channel_id=1, source_target_pairs={{0,128},{8,40},{16,144},{24,56},{32,160},{40,8},{48,176},{56,24},{... | collective-permute-start | bytes 614408 | tf_op jit(solution)/shard_map/ppermute | solution.py:60
